TPU v7x, 128 devices: a whole 4x4x4 slice. The times are simulated.
128 devices in a mesh: dp: 4 (over x), tensor: 4 (over y_hi, core), context: 8 (over y_lo, z).
Axes of the slice: x: 4, y: 4 (y_hi: 2, y_lo: 2; y = y_hi * 2 + y_lo), z: 4, core: 2. Of those that a mesh axis runs over, the one named last changes fastest.
Arguments:
- tokens: bfloat16 [16384, 4096], P(('dp', 'tensor', 'context')), may hold values from -6 to 6
- routes: int32 [16384, 2], P(('dp', 'tensor', 'context')), may hold values from 0 to 31, all different within a row; in each aligned block of 128 rows (0 to 127, 128 to 255, ...) at most 10 rows name the same one
- gates: float32 [16384, 2], P(('dp', 'tensor', 'context')), may hold values from 0.1 to 1
- cotangent: bfloat16 [16384, 4096], P(('dp', 'tensor', 'context')), may hold values from -3 to 3
- w_gate: bfloat16 [32, 4096, 768], P(('tensor', 'context'), 'dp'), may hold values from -0.09375 to 0.09375
- w_up: bfloat16 [32, 4096, 768], P(('tensor', 'context'), 'dp'), may hold values from -0.09375 to 0.09375
- w_down: bfloat16 [32, 768, 4096], P(('tensor', 'context'), None, 'dp'), may hold values from -0.21875 to 0.21875
Outputs:
- mixed: bfloat16 [16384, 4096], P(('dp', 'tensor', 'context'))
- d_tokens: bfloat16 [16384, 4096], P(('dp', 'tensor', 'context'))
- grad_gate: bfloat16 [32, 4096, 768], P(('tensor', 'context'), 'dp')
- grad_up: bfloat16 [32, 4096, 768], P(('tensor', 'context'), 'dp')
- grad_down: bfloat16 [32, 768, 4096], P(('tensor', 'context'), None, 'dp')
Inputs may be any that keep to these rules, and one draw needn't show every extreme that they name: `routes`: each row names 2 different experts; within the rows of one device no expert is named more than 10 times, a bound that some block reaches.
All inputs are finite; a program needn't handle non-finite values.
Results may differ from a plain program's by a relative error of at most 0.023.
Values may be sent and summed in bfloat16 or wider, within the bound.
A program may use at most 128 MiB of HBM per device.

v0:
```python
import jax
import jax.numpy as jnp
from jax import lax
from jax.sharding import PartitionSpec as P


def slot_tables(routes, gates, experts, cap):
    tok, top = routes.shape
    pairs = tok * top
    flat_exp = routes.reshape(pairs)
    chosen = (flat_exp[:, None] == jnp.arange(experts, dtype=jnp.int32)[None, :]).astype(jnp.int32)
    before = jnp.cumsum(chosen, axis=0) - chosen
    slot = jnp.sum(before * chosen, axis=1)
    dest = flat_exp * cap + slot
    match = (dest[None, :] == jnp.arange(experts * cap, dtype=jnp.int32)[:, None]).astype(jnp.int32)
    filled = jnp.sum(match, axis=1)
    owner = jnp.sum(match * jnp.arange(pairs, dtype=jnp.int32)[None, :], axis=1) // top
    weight = jnp.sum(match.astype(jnp.float32) * gates.reshape(pairs)[None, :], axis=1)
    return (dest, owner, filled, weight)


def expert_pass(x_rows, dy_rows, w_gate, w_up, w_down):
    gate_h = jnp.dot(x_rows, w_gate, preferred_element_type=jnp.float32)
    up_h = jnp.dot(x_rows, w_up, preferred_element_type=jnp.float32)
    sigma = jax.nn.sigmoid(gate_h)
    active = gate_h * sigma
    hidden = (active * up_h).astype(jnp.bfloat16)
    y_rows = jnp.dot(hidden, w_down, preferred_element_type=jnp.float32).astype(jnp.bfloat16)
    d_hidden = jnp.dot(dy_rows, w_down.T, preferred_element_type=jnp.float32)
    d_gate = (d_hidden * up_h * sigma * (1.0 + gate_h * (1.0 - sigma))).astype(jnp.bfloat16)
    d_up = (d_hidden * active).astype(jnp.bfloat16)
    dx_rows = (
        jnp.dot(d_gate, w_gate.T, preferred_element_type=jnp.float32)
        + jnp.dot(d_up, w_up.T, preferred_element_type=jnp.float32)
    ).astype(jnp.bfloat16)
    g_gate = jnp.dot(x_rows.T, d_gate, preferred_element_type=jnp.float32)
    g_up = jnp.dot(x_rows.T, d_up, preferred_element_type=jnp.float32)
    g_down = jnp.dot(hidden.T, dy_rows, preferred_element_type=jnp.float32)
    return (y_rows, dx_rows, g_gate, g_up, g_down)


def shards(tokens, routes, gates, cotangent, w_gate, w_up, w_down):
    n_tensor = lax.axis_size("tensor")
    n_context = lax.axis_size("context")
    experts = n_tensor * n_context
    tok, top = routes.shape
    width = tokens.shape[1]
    cap = max(2, tok * top * 5 // (4 * experts))
    dest, owner, filled, weight = slot_tables(routes, gates, experts, cap)
    picked = jnp.take(tokens, owner, axis=0)
    x_send = jnp.where((filled > 0)[:, None], picked, jnp.zeros_like(picked))
    dy_send = (weight[:, None] * jnp.take(cotangent, owner, axis=0).astype(jnp.float32)).astype(
        jnp.bfloat16
    )

    def route(buffer):
        depth = buffer.shape[1]
        shaped = buffer.reshape(experts, cap, depth)
        moved = lax.all_to_all(
            shaped, ("tensor", "context"), split_axis=0, concat_axis=0, tiled=True
        )
        return moved.reshape(experts * cap, depth)

    x_rows = route(x_send)
    dy_rows = route(dy_send)
    wg = w_gate[0]
    wu = w_up[0]
    wd = w_down[0]
    full_gate, full_up, full_down = (
        lax.all_gather(wg, "dp", axis=0, tiled=True),
        lax.all_gather(wu, "dp", axis=0, tiled=True),
        lax.all_gather(wd, "dp", axis=1, tiled=True),
    )
    y_rows, dx_rows, g_gate, g_up, g_down = expert_pass(
        x_rows, dy_rows, full_gate, full_up, full_down
    )
    s_gate, s_up, s_down = (
        lax.psum_scatter(g_gate.astype(jnp.bfloat16), "dp", scatter_dimension=0, tiled=True).astype(
            jnp.float32
        ),
        lax.psum_scatter(g_up.astype(jnp.bfloat16), "dp", scatter_dimension=0, tiled=True).astype(
            jnp.float32
        ),
        lax.psum_scatter(g_down.astype(jnp.bfloat16), "dp", scatter_dimension=1, tiled=True).astype(
            jnp.float32
        ),
    )
    grad_gate = s_gate.astype(jnp.bfloat16)
    grad_up = s_up.astype(jnp.bfloat16)
    grad_down = s_down.astype(jnp.bfloat16)
    y_back = route(y_rows)
    dx_back = route(dx_rows)
    y_taken = jnp.take(y_back, dest, axis=0).reshape(tok, top, width).astype(jnp.float32)
    mixed = jnp.sum(gates[:, :, None] * y_taken, axis=1).astype(jnp.bfloat16)
    dx_taken = jnp.take(dx_back, dest, axis=0).reshape(tok, top, width).astype(jnp.float32)
    d_tokens = jnp.sum(dx_taken, axis=1).astype(jnp.bfloat16)
    return (mixed, d_tokens, grad_gate[None], grad_up[None], grad_down[None])


def solution(mesh):
    placed = (
        P(("dp", "tensor", "context"), None),
        P(("dp", "tensor", "context"), None),
        P(("dp", "tensor", "context"), None),
        P(("dp", "tensor", "context"), None),
        P(("tensor", "context"), "dp", None),
        P(("tensor", "context"), "dp", None),
        P(("tensor", "context"), None, "dp"),
    )
    return jax.shard_map(
        shards,
        mesh=mesh,
        in_specs=placed,
        out_specs=(
            P(("dp", "tensor", "context"), None),
            P(("dp", "tensor", "context"), None),
            P(("tensor", "context"), "dp", None),
            P(("tensor", "context"), "dp", None),
            P(("tensor", "context"), None, "dp"),
        ),
        check_vma=False,
    )
```

profile of v0, /device:TPU:1, one launch (start us, length us, event | category | flops | bytes accessed | tf_op | source)
XLA Modules:
  0.0 433.2 jit_solution(14693463401103630198)
XLA Ops:
  7.2 0.7 all-gather.9.cloned.1.call-update
  8.0 0.7 all-gather.11.cloned.1.call-update
  8.7 0.7 all-gather.7.cloned.1.call-update
  9.8 0.6 reduce-window.6
  10.4 0.2 slice_reduce_fusion
  10.8 0.2 convert_reduce_fusion
  11.0 3.9 gather_fusion
  14.9 2.1 select_select_fusion
  17.0 2.8 reshape.86
  19.8 9.8 %all-to-all-start = ((bf16[32,10,4096]{2,1,0:T(8,128)(2,1)}), bf16[32,10,4096]{2,1,0:T(8,128)(2,1)}, u32[]{:S(2)}, u32[]{:S(2)}) async-start(bf16[32,10,4096]{2,1,0:T(8,128)(2,1)} %reshape.86), calls=%async_computation | async-start | bytes 8388608 | tf_op jit(solution)/shard_map/all_to_all | solution.py:59
  29.6 3.9 gather_fusion.2
  33.7 0.2 fusion.23
  33.9 3.0 multiply_convert_fusion
  36.9 2.8 reshape.90
  39.7 41.5 %all-to-all-done = bf16[32,10,4096]{2,1,0:T(8,128)(2,1)} async-done(((bf16[32,10,4096]{2,1,0:T(8,128)(2,1)}), bf16[32,10,4096]{2,1,0:T(8,128)(2,1)}, u32[]{:S(2)}, u32[]{:S(2)}) %all-to-all-start) | async-done | bytes 2621472 | tf_op jit(solution)/shard_map/all_to_all | solution.py:59
  81.2 7.4 %all-to-all-start.2 = ((bf16[32,10,4096]{2,1,0:T(8,128)(2,1)}), bf16[32,10,4096]{2,1,0:T(8,128)(2,1)}, u32[]{:S(2)}, u32[]{:S(2)}) async-start(bf16[32,10,4096]{2,1,0:T(8,128)(2,1)} %reshape.90), calls=%async_computation.2 | async-start | bytes 8388608 | tf_op jit(solution)/shard_map/all_to_all | solution.py:59
  88.6 0.5 reduce-scatter.4.cloned.1.call-start
  89.1 5.0 %reshape.87 = bf16[320,4096]{1,0:T(8,128)(2,1)} reshape(bf16[32,10,4096]{2,1,0:T(8,128)(2,1)} %all-to-all-done) | data formatting | bytes 5242880 | tf_op jit(solution)/shard_map/reshape | solution.py:62
  94.1 46.1 %all-to-all-done.2 = bf16[32,10,4096]{2,1,0:T(8,128)(2,1)} async-done(((bf16[32,10,4096]{2,1,0:T(8,128)(2,1)}), bf16[32,10,4096]{2,1,0:T(8,128)(2,1)}, u32[]{:S(2)}, u32[]{:S(2)}) %all-to-all-start.2) | async-done | bytes 2621472 | tf_op jit(solution)/shard_map/all_to_all | solution.py:59
  140.1 3.3 reshape.91
  143.5 6.7 %fusion.6 = f32[320,768]{1,0:T(8,128)} fusion(bf16[320,4096]{1,0:T(8,128)(2,1)} %reshape.87, bf16[1,4096,768]{2,1,0:T(8,128)(2,1)} %all-gather.9.cloned.1.call-done), kind=kOutput, calls=%fused_computation.13 | convolution fusion | flops 2013265920 | bytes 9895936 | tf_op jit(solution)/shard_map/dot_general | solution.py:24
  150.2 6.0 %fusion = f32[320,768]{1,0:T(8,128)} fusion(bf16[320,4096]{1,0:T(8,128)(2,1)S(1)} %reshape.91, bf16[1,768,4096]{2,1,0:T(8,128)(2,1)} %all-gather.11.cloned.1.call-done), kind=kOutput, calls=%fused_computation.7 | convolution fusion | flops 2013265920 | bytes 9895936 | tf_op jit(solution)/shard_map/dot_general | solution.py:29
  156.2 58.5 %all-gather.7.cloned.1.call-done = bf16[1,4096,768]{2,1,0:T(8,128)(2,1)} async-done(((bf16[1,1024,768]{2,1,0:T(8,128)(2,1)}), bf16[1,4096,768]{2,1,0:T(8,128)(2,1)}) %all-gather.7.cloned.1.call-update) | async-done | bytes 6291472 | tf_op jit(solution)/shard_map/all_gather | solution.py:70
  214.6 7.5 %multiply_convert_fusion.2 = (bf16[320,768]{1,0:T(8,128)(2,1)S(1)}, bf16[320,768]{1,0:T(8,128)(2,1)S(1)}, bf16[320,768]{1,0:T(8,128)(2,1)}) fusion(f32[320,768]{1,0:T(8,128)} %fusion, f32[320,768]{1,0:T(8,128)} %fusion.6, bf16[320,4096]{1,0:T(8,128)(2,1)} %reshape.87, bf16[1,4096,768]{2,1,0:T(8,128)(2,1)} %all-gather.7.cloned.1.call-done), kind=kOutput, calls=%fused_computation.28 | convolution fusion | flops 2016952320 | bytes 12353536 | tf_op jit(solution)/shard_map/dot_general | solution.py:23
  222.1 0.8 copy-done.6
  222.9 5.4 %convolution_convert_fusion.2 = bf16[4096,768]{1,0:T(8,128)(2,1)} fusion(bf16[320,4096]{1,0:T(8,128)(2,1)S(1)} %copy-done.3, bf16[320,768]{1,0:T(8,128)(2,1)S(1)} %get-tuple-element.13), kind=kOutput, calls=%fused_computation.6 | convolution fusion | flops 2016411648 | bytes 9404416 | tf_op jit(solution)/shard_map/dot_general | solution.py:36
  228.3 7.9 %convolution_convert_fusion.1 = bf16[4096,768]{1,0:T(8,128)(2,1)} fusion(bf16[320,4096]{1,0:T(8,128)(2,1)} %reshape.87, bf16[320,768]{1,0:T(8,128)(2,1)S(1)} %get-tuple-element.14), kind=kOutput, calls=%fused_computation.5 | convolution fusion | flops 2016411648 | bytes 9404416 | tf_op jit(solution)/shard_map/dot_general | solution.py:37
  236.2 0.2 reduce-scatter.8.cloned.1.call-start
  236.4 6.5 %convolution_convert_fusion = bf16[768,4096]{1,0:T(8,128)(2,1)} fusion(bf16[320,768]{1,0:T(8,128)(2,1)} %get-tuple-element.15, bf16[320,4096]{1,0:T(8,128)(2,1)S(1)} %reshape.91), kind=kOutput, calls=%fused_computation.4 | convolution fusion | flops 2016411648 | bytes 9404416 | tf_op jit(solution)/shard_map/dot_general | solution.py:38
  243.0 5.1 %fusion.4 = f32[320,4096]{1,0:T(8,128)S(1)} fusion(bf16[320,768]{1,0:T(8,128)(2,1)S(1)} %get-tuple-element.14, bf16[1,4096,768]{2,1,0:T(8,128)(2,1)} %all-gather.9.cloned.1.call-done), kind=kOutput, calls=%fused_computation.11 | convolution fusion | flops 2013265920 | bytes 12025856 | tf_op jit(solution)/shard_map/dot_general | solution.py:34
  248.0 5.1 %fusion.15 = bf16[320,4096]{1,0:T(8,128)(2,1)S(1)} fusion(f32[320,4096]{1,0:T(8,128)S(1)} %fusion.4, bf16[320,768]{1,0:T(8,128)(2,1)S(1)} %copy-done.7, bf16[1,4096,768]{2,1,0:T(8,128)(2,1)} %all-gather.7.cloned.1.call-done), kind=kOutput, calls=%fused_computation.20 | convolution fusion | flops 2015887360 | bytes 14647296 | tf_op jit(solution)/shard_map/dot_general | solution.py:33
  253.1 2.8 reshape.92
  255.9 7.9 %all-to-all-start.3 = ((bf16[32,10,4096]{2,1,0:T(8,128)(2,1)}), bf16[32,10,4096]{2,1,0:T(8,128)(2,1)}, u32[]{:S(2)}, u32[]{:S(2)}) async-start(bf16[32,10,4096]{2,1,0:T(8,128)(2,1)} %reshape.92), calls=%async_computation.3 | async-start | bytes 8388608 | tf_op jit(solution)/shard_map/all_to_all | solution.py:59
  263.9 5.0 %fusion.18 = bf16[320,4096]{1,0:T(8,128)(2,1)S(1)} fusion(bf16[320,768]{1,0:T(8,128)(2,1)S(1)} %copy-done.8, bf16[1,768,4096]{2,1,0:T(8,128)(2,1)} %all-gather.11.cloned.1.call-done), kind=kOutput, calls=%fused_computation.21 | convolution fusion | flops 2014576640 | bytes 9404416 | tf_op jit(solution)/shard_map/dot_general | solution.py:28
  268.9 2.8 reshape.88
  271.7 43.7 %all-to-all-done.3 = bf16[32,10,4096]{2,1,0:T(8,128)(2,1)} async-done(((bf16[32,10,4096]{2,1,0:T(8,128)(2,1)}), bf16[32,10,4096]{2,1,0:T(8,128)(2,1)}, u32[]{:S(2)}, u32[]{:S(2)}) %all-to-all-start.3) | async-done | bytes 2621472 | tf_op jit(solution)/shard_map/all_to_all | solution.py:59
  315.4 7.4 %all-to-all-start.1 = ((bf16[32,10,4096]{2,1,0:T(8,128)(2,1)}), bf16[32,10,4096]{2,1,0:T(8,128)(2,1)}, u32[]{:S(2)}, u32[]{:S(2)}) async-start(bf16[32,10,4096]{2,1,0:T(8,128)(2,1)} %reshape.88), calls=%async_computation.1 | async-start | bytes 8388608 | tf_op jit(solution)/shard_map/all_to_all | solution.py:59
  322.9 3.3 reshape.93
  326.2 3.2 gather_fusion.3
  329.4 45.0 %all-to-all-done.1 = bf16[32,10,4096]{2,1,0:T(8,128)(2,1)} async-done(((bf16[32,10,4096]{2,1,0:T(8,128)(2,1)}), bf16[32,10,4096]{2,1,0:T(8,128)(2,1)}, u32[]{:S(2)}, u32[]{:S(2)}) %all-to-all-start.1) | async-done | bytes 2621472 | tf_op jit(solution)/shard_map/all_to_all | solution.py:59
  374.4 3.3 reshape.89
  377.7 3.2 gather_fusion.1
  380.9 5.3 %broadcast_select_fusion = (bf16[256,4096]{1,0:T(8,128)(2,1)}, f32[256,4096]{1,0:T(8,128)}) fusion(bf16[256,4096]{1,0:T(8,128)(2,1)} %gather_fusion.3, pred[256]{0:T(512)(128)(4,1)S(1)} %get-tuple-element.9, bf16[256,4096]{1,0:T(8,128)(2,1)} %gather_fusion.1), kind=kLoop, calls=%fused_computation.26 | loop fusion | flops 3145728 | bytes 10486016 | tf_op jit(solution)/shard_map/jit(_take)/select_n | solution.py:95
  386.2 5.8 %reshape.95 = f32[128,2,4096]{2,1,0:T(2,128)} reshape(f32[256,4096]{1,0:T(8,128)} %get-tuple-element.17) | data formatting | bytes 8388608 | tf_op jit(solution)/shard_map/convert_element_type | solution.py:93
  392.1 3.4 reshape.94
  395.5 7.2 %reduce_sum.62 = bf16[128,4096]{1,0:T(8,128)(2,1)} reduce(bf16[128,2,4096]{2,1,0:T(2,128)(2,1)S(1)} %reshape.94, bf16[]{:T(256)} %constant.47.clone.1), dimensions={1}, to_apply=%region_7.10 | reduce | flops 524288 | bytes 3145730 | tf_op jit(solution)/shard_map/reduce_sum | solution.py:96
  402.7 9.6 %multiply_reduce_fusion = bf16[128,4096]{1,0:T(8,128)(2,1)} fusion(f32[128,2,4096]{2,1,0:T(2,128)} %reshape.95, f32[128,2]{1,0:T(8,128)S(1)} %copy.18), kind=kLoop, calls=%fused_computation.23 | loop fusion | flops 1572864 | bytes 5243904 | tf_op jit(solution)/shard_map/reduce_sum | solution.py:94
  412.3 13.8 %reduce-scatter.8.cloned.1.call-done = bf16[768,1024]{1,0:T(8,128)(2,1)} async-done(((bf16[768,4096]{1,0:T(8,128)(2,1)}), bf16[768,1024]{1,0:T(8,128)(2,1)}) %reduce-scatter.8.cloned.1.call-update) | async-done | bytes 1572880 | tf_op jit(solution)/shard_map/reduce_scatter | solution.py:84
  (42 shorter events, 1.1 us)
Async XLA Ops:
  7.2 3.8 copy-start
  7.2 2.2 copy-start.4
  7.2 136.3 %all-gather.9.cloned.1.call-start = ((), (), s32[]{:S(2)}) async-start(), calls=%async_computation.11 | async-start | bytes 7864320 | tf_op jit(solution)/shard_map/all_gather | solution.py:71
  7.9 142.3 %all-gather.11.cloned.1.call-start = ((), (), s32[]{:S(2)}) async-start(), calls=%async_computation.12 | async-start | bytes 7864320 | tf_op jit(solution)/shard_map/all_gather | solution.py:72
  8.7 206.0 %all-gather.7.cloned.1.call-start = ((), (), s32[]{:S(2)}) async-start(), calls=%async_computation.10 | async-start | bytes 7864320 | tf_op jit(solution)/shard_map/all_gather | solution.py:70
  19.8 9.8 %copy-start.2 = (bf16[128,4096]{1,0:T(8,128)(2,1)S(1)}, bf16[128,4096]{1,0:T(8,128)(2,1)}, u32[]{:S(2)}) copy-start(bf16[128,4096]{1,0:T(8,128)(2,1)} %param.14) | copy-start | bytes 3145732
  19.8 61.4 %all-to-all-start = ((bf16[32,10,4096]{2,1,0:T(8,128)(2,1)}), bf16[32,10,4096]{2,1,0:T(8,128)(2,1)}, u32[]{:S(2)}, u32[]{:S(2)}) async-start(bf16[32,10,4096]{2,1,0:T(8,128)(2,1)} %reshape.86), calls=%async_computation | async-start | bytes 8388608 | tf_op jit(solution)/shard_map/all_to_all | solution.py:59
  29.6 3.9 copy-start.5
  81.2 58.9 %all-to-all-start.2 = ((bf16[32,10,4096]{2,1,0:T(8,128)(2,1)}), bf16[32,10,4096]{2,1,0:T(8,128)(2,1)}, u32[]{:S(2)}, u32[]{:S(2)}) async-start(bf16[32,10,4096]{2,1,0:T(8,128)(2,1)} %reshape.90), calls=%async_computation.2 | async-start | bytes 8388608 | tf_op jit(solution)/shard_map/all_to_all | solution.py:59
  88.6 323.8 %reduce-scatter.4.cloned.1.call-start = ((), (), s32[]{:S(2)}) async-start(), calls=%async_computation.7 | async-start | bytes 7864320 | tf_op jit(solution)/shard_map/reduce_scatter | solution.py:78
  214.6 8.2 %copy-start.3 = (bf16[320,4096]{1,0:T(8,128)(2,1)S(1)}, bf16[320,4096]{1,0:T(8,128)(2,1)}, u32[]{:S(2)}) copy-start(bf16[320,4096]{1,0:T(8,128)(2,1)} %reshape.87) | copy-start | bytes 7864324
  222.1 0.8 copy-start.6
  228.3 184.1 %reduce-scatter.6.cloned.1.call-start = ((), (), s32[]{:S(2)}) async-start(), calls=%async_computation.8 | async-start | bytes 7864320 | tf_op jit(solution)/shard_map/reduce_scatter | solution.py:81
  236.2 189.9 %reduce-scatter.8.cloned.1.call-start = ((), (), s32[]{:S(2)}) async-start(), calls=%async_computation.9 | async-start | bytes 7864320 | tf_op jit(solution)/shard_map/reduce_scatter | solution.py:84
  242.9 5.1 %copy-start.7 = (bf16[320,768]{1,0:T(8,128)(2,1)S(1)}, bf16[320,768]{1,0:T(8,128)(2,1)}, u32[]{:S(2)}) copy-start(bf16[320,768]{1,0:T(8,128)(2,1)} %copy-done.6) | copy-start | bytes 1474564
  255.9 7.9 %copy-start.8 = (bf16[320,768]{1,0:T(8,128)(2,1)S(1)}, bf16[320,768]{1,0:T(8,128)(2,1)}, u32[]{:S(2)}) copy-start(bf16[320,768]{1,0:T(8,128)(2,1)} %get-tuple-element.15) | copy-start | bytes 1474564
  255.9 59.5 %all-to-all-start.3 = ((bf16[32,10,4096]{2,1,0:T(8,128)(2,1)}), bf16[32,10,4096]{2,1,0:T(8,128)(2,1)}, u32[]{:S(2)}, u32[]{:S(2)}) async-start(bf16[32,10,4096]{2,1,0:T(8,128)(2,1)} %reshape.92), calls=%async_computation.3 | async-start | bytes 8388608 | tf_op jit(solution)/shard_map/all_to_all | solution.py:59
  315.4 58.9 %all-to-all-start.1 = ((bf16[32,10,4096]{2,1,0:T(8,128)(2,1)}), bf16[32,10,4096]{2,1,0:T(8,128)(2,1)}, u32[]{:S(2)}, u32[]{:S(2)}) async-start(bf16[32,10,4096]{2,1,0:T(8,128)(2,1)} %reshape.88), calls=%async_computation.1 | async-start | bytes 8388608 | tf_op jit(solution)/shard_map/all_to_all | solution.py:59
  395.5 30.6 %copy-start.1 = (bf16[128,4096]{1,0:T(8,128)(2,1)S(1)}, bf16[128,4096]{1,0:T(8,128)(2,1)}, u32[]{:S(2)}) copy-start(bf16[128,4096]{1,0:T(8,128)(2,1)} %param.11) | copy-start | bytes 3145732
Sparse Core Ops, SparseCore 0:
  9.7 68.8 all-gather.8
  80.2 66.3 all-gather.10
  148.3 66.3 all-gather.6
  228.4 64.6 reduce-scatter.3
  295.9 63.6 reduce-scatter.5
  362.4 63.6 reduce-scatter.7
where the time goes:
time: 439 us; the launch traced here: 433 us
  waiting for transfers between devices  251 us (57%)
  matrix products  55 us (13%)
  local copies, waits for them, and re-layouts  51.1 us (12%)
  starting transfers between devices  33.3 us (8%)
  other arithmetic  28.4 us (6%)
  between operations  14.6 us (3%)
    all_to_all x4, waiting for transfers between devices, route(): lax.all_to_all(shaped, ('tensor', 'context'), split_axis=0, concat_axis=0...  176 us
    all_gather x1, waiting for transfers between devices, shards(): lax.all_gather(wg, 'dp', axis=0, tiled=True)  58.5 us
    all_to_all x4, starting transfers between devices, route(): lax.all_to_all(shaped, ('tensor', 'context'), split_axis=0, concat_axis=0...  32.5 us
    reshape x4, local copies, waits for them, and re-layouts, route(): return moved.reshape(experts * cap, depth)  14.9 us
    reduce_scatter x1, waiting for transfers between devices, shards(): lax.psum_scatter(g_down.astype(jnp.bfloat16), 'dp', scatter_dimension=1,...  13.8 us
    reshape x4, local copies, waits for them, and re-layouts, route(): shaped = buffer.reshape(experts, cap, depth)  11.2 us
    reduce_sum x1, other arithmetic, shards(): mixed = jnp.sum(gates[:, :, None] * y_taken, axis=1).astype(jnp.bfloat16)  9.64 us
  transfers between devices with their start and end apart: 10, of which 6 were waited for; matrix products, arithmetic and copies ran while one was open for 28% of the time, Pallas kernels for 0%

commit v1 on v0

v1 whole, which is shorter than its diff:
```python
import functools

import jax
import jax.numpy as jnp
from jax import lax
from jax.experimental import pallas as pl
from jax.experimental.pallas import tpu as pltpu
from jax.sharding import PartitionSpec as P

MESH = pl.DeviceIdType.MESH
GROUPS = 4
EXPERTS = 32
CAP = 10
TOK = 128
SLAB = GROUPS * CAP
CHUNKS = 4
PER = EXPERTS // CHUNKS
ROWS = PER * SLAB
OWN = ROWS // GROUPS
SELF = 8

NT = (((1,), (1,)), ((), ()))
TN = (((0,), (0,)), ((), ()))


def dot(a, b):
    return jnp.dot(a, b, preferred_element_type=jnp.float32)


def kernel(
    tab_ref, tokens, cotangent, w_gate, w_up, w_down,
    mixed, d_tokens, g_gate, g_up, g_down,
    tb, tx, tc, oh, og, wg, wu, wd, sx, sy, rx, ry, by, bx, xs, ys, part, got, act, gu, gg,
    tab_s, tab_r, tx_s, tx_r, tc_s, tc_r, loc,
    sx_s, sx_r, sy_s, sy_r, bks_y, bkr_y, bks_x, bkr_x,
    rs1_s, rs1_r, rs2_s, rs2_r, ag1_s, ag1_r, ag2_s, ag2_r,
    fm_s, fm_r, fd_s, fd_r,
):
    d = lax.axis_index("dp")
    t = lax.axis_index("tensor")
    c = lax.axis_index("context")
    core = lax.rem(t, 2)
    py = (t // 2) * 2 + c // 4
    pz = lax.rem(c, 4)
    width = tx.shape[2]
    half = width // 2

    def offset(j):
        kpos, i = j // PER, lax.rem(j, PER)
        kk = lax.rem(2 + 2 * kpos + (kpos // 2) * 3, 4)
        z = lax.rem(i, 4)
        return i // 4, lax.rem(kk + 4 - z, 4), z

    def peer(j, sign):
        a, y, z = offset(j)
        if sign < 0:
            y, z = 4 - y, 4 - z
        y, z = lax.rem(py + y, 4), lax.rem(pz + z, 4)
        return (d, (y // 2) * 2 + lax.rem(core + a, 2), lax.rem(y, 2) * 4 + z)

    def ring(p):
        return (lax.rem(d + p, GROUPS), t, c)

    def remote(src, dst, s, r, dev):
        return pltpu.make_async_remote_copy(
            src_ref=src, dst_ref=dst, send_sem=s, recv_sem=r, device_id=dev, device_id_type=MESH
        )

    barrier = pltpu.get_barrier_semaphore()

    def greet(j, carry):
        @pl.when(j != SELF)
        def _():
            pl.semaphore_signal(barrier, inc=1, device_id=peer(j, 1), device_id_type=MESH)

        return carry

    lax.fori_loop(0, EXPERTS, greet, 0)
    for p in range(1, GROUPS):
        pl.semaphore_signal(barrier, inc=1, device_id=ring(p), device_id_type=MESH)
    pl.semaphore_wait(barrier, EXPERTS - 1 + GROUPS - 1)

    def columns(p):
        q = lax.rem(d + p, GROUPS)
        return pl.ds(pl.multiple_of(q * width, width), width)

    def dense(src, dst, s, r, p):
        return remote(src.at[:, columns(p)], dst.at[d], s.at[p - 1], r.at[p - 1], ring(p))

    own_tx = pltpu.make_async_copy(tokens.at[:, columns(0)], tx.at[d], loc.at[0])
    own_tc = pltpu.make_async_copy(cotangent.at[:, columns(0)], tc.at[d], loc.at[1])
    for p in range(1, GROUPS):
        dense(tokens, tx, tx_s, tx_r, p).start()
    own_tx.start()
    for p in range(1, GROUPS):
        dense(cotangent, tc, tc_s, tc_r, p).start()
    own_tc.start()
    weights = [
        pltpu.make_async_copy(w_gate.at[0], wg, loc.at[2]),
        pltpu.make_async_copy(w_up.at[0], wu, loc.at[3]),
        pltpu.make_async_copy(w_down.at[0], wd, loc.at[4]),
    ]
    for w in weights:
        w.start()

    e = lax.broadcasted_iota(jnp.int32, (EXPERTS, TOK), 0)
    e_core = (e >> 3) & 1
    e_y = (e >> 4) * 2 + ((e >> 2) & 1)
    e_z = e & 3
    oa = (e_core - core + 2) & 1
    oy = (e_y - py + 4) & 3
    oz = (e_z - pz + 4) & 3
    kk = (oy + oz) & 3
    kpos = jnp.where(kk == 2, 0, jnp.where(kk == 0, 1, jnp.where(kk == 1, 2, 3)))
    first_row = ((kpos * PER + oa * 4 + oz) * SLAB + d * CAP).astype(jnp.float32)
    e_f = e.astype(jnp.float32)
    tab = tab_ref[...]
    chosen0 = jnp.where(e_f == tab[0:1, :], 1.0, 0.0)
    chosen1 = jnp.where(e_f == tab[1:2, :], 1.0, 0.0)
    earlier = jnp.where(
        lax.broadcasted_iota(jnp.int32, (TOK, TOK), 0) < lax.broadcasted_iota(jnp.int32, (TOK, TOK), 1), 1.0, 0.0
    ).astype(jnp.bfloat16)
    before = dot((chosen0 + chosen1).astype(jnp.bfloat16), earlier)
    place = first_row + before
    key0 = jnp.sum(chosen0 * place, axis=0, keepdims=True)
    key1 = jnp.sum(chosen1 * place, axis=0, keepdims=True)
    tb[d] = jnp.concatenate([key0, key1, tab[2:4, :], jnp.zeros((4, TOK), jnp.float32)], axis=0)

    def tables(p):
        return remote(tb.at[d], tb.at[d], tab_s.at[p - 1], tab_r.at[p - 1], ring(p))

    for p in range(1, GROUPS):
        tables(p).start()
    for p in range(1, GROUPS):
        tables(p).wait()

    def halves(value):
        return [value[:, h * half : (h + 1) * half].reshape(PER, SLAB, half) for h in range(2)]

    def to_slabs(buf, k, value):
        for h, v in enumerate(halves(value)):
            buf[pl.ds(k * PER, PER), h * SLAB : (h + 1) * SLAB, :] = v.astype(jnp.bfloat16)

    def from_slabs(buf, k, h):
        v = buf[pl.ds(k * PER, PER), h * SLAB : (h + 1) * SLAB, :].astype(jnp.float32)
        return v.reshape(ROWS, half).astype(jnp.bfloat16)

    def slab_copy(src, dst, s, r, j, sign):
        return remote(src.at[j], dst.at[j], s.at[j], r.at[j], peer(j, sign))

    def each_slot(k, act_on):
        def body(i, carry):
            j = k * PER + i

            @pl.when(j != SELF)
            def _():
                act_on(j)

            return carry

        lax.fori_loop(0, PER, body, 0)

    def send_slabs(src, dst, s, r, k, sign):
        each_slot(k, lambda j: slab_copy(src, dst, s, r, j, sign).start())

        @pl.when(k == SELF // PER)
        def _():
            dst[SELF] = src[SELF]

    def await_slabs(src, dst, s, r, k, sign):
        each_slot(k, lambda j: slab_copy(src, dst, s, r, j, sign).wait_recv())

    def await_sent(src, dst, s, r, k, sign):
        each_slot(k, lambda j: slab_copy(src, dst, s, r, j, sign).wait_send())

    for p in range(1, GROUPS):
        dense(tokens, tx, tx_s, tx_r, p).wait()
    own_tx.wait()

    def send_x(k, carry):
        row = (lax.broadcasted_iota(jnp.int32, (ROWS, TOK), 0) + k * ROWS).astype(jnp.float32)
        for g in range(GROUPS):
            info = tb[g]
            hit0, hit1 = row == info[0:1, :], row == info[1:2, :]
            cols = slice(g * TOK, (g + 1) * TOK)
            oh[k, :, cols] = jnp.where(hit0 | hit1, 1.0, 0.0).astype(jnp.bfloat16)
            og[k, :, cols] = jnp.where(hit0, info[2:3, :], jnp.where(hit1, info[3:4, :], 0.0))
        to_slabs(sx, k, dot(oh[k], tx[...].reshape(GROUPS * TOK, width)))
        send_slabs(sx, rx, sx_s, sx_r, k, 1)
        return carry

    lax.fori_loop(0, CHUNKS, send_x, 0)

    for p in range(1, GROUPS):
        dense(cotangent, tc, tc_s, tc_r, p).wait()
    own_tc.wait()

    def send_dy(k, carry):
        weight = jnp.sum(og[k], axis=1, keepdims=True)
        to_slabs(sy, k, dot(oh[k], tc[...].reshape(GROUPS * TOK, width)) * weight)
        send_slabs(sy, ry, sy_s, sy_r, k, 1)
        return carry

    lax.fori_loop(0, CHUNKS, send_dy, 0)
    for w in weights:
        w.wait()

    def rs1(k, p):
        q = lax.rem(d + p, GROUPS)
        return remote(
            part.at[k, q, pl.ds(0, 2)], got.at[k, p - 1, pl.ds(0, 2)], rs1_s.at[k, p - 1], rs1_r.at[k, p - 1], ring(p)
        )

    def rs2(k, p):
        q = lax.rem(d + p, GROUPS)
        return remote(part.at[k, q, 2], got.at[k, p - 1, 2], rs2_s.at[k, p - 1], rs2_r.at[k, p - 1], ring(p))

    def ag1(k, p):
        return remote(act.at[0, k, d], act.at[0, k, d], ag1_s.at[k, p - 1], ag1_r.at[k, p - 1], ring(p))

    def ag2(k, p):
        own = act.at[pl.ds(1, 2), k, d]
        return remote(own, own, ag2_s.at[k, p - 1], ag2_r.at[k, p - 1], ring(p))

    def partial_sums(k, q, value):
        part[k, :, q] = value.astype(jnp.bfloat16).reshape(GROUPS, OWN, value.shape[1])

    def first(k, carry):
        await_slabs(sx, rx, sx_s, sx_r, k, 1)
        for h in range(2):
            xs[k, :, h * half : (h + 1) * half] = from_slabs(rx, k, h)
        partial_sums(k, 0, dot(xs[k], wg[...]))
        partial_sums(k, 1, dot(xs[k], wu[...]))
        for p in range(1, GROUPS):
            rs1(k, p).start()
        return carry

    lax.fori_loop(0, CHUNKS, first, 0)

    def reduced(k, q):
        total = part[k, d, q].astype(jnp.float32)
        for p in range(1, GROUPS):
            total += got[k, p - 1, q].astype(jnp.float32)
        return total

    def second(k, carry):
        for p in range(1, GROUPS):
            rs1(k, p).wait()
        gate_h, up_h = reduced(k, 0), reduced(k, 1)
        gu[k, 0] = gate_h
        gu[k, 1] = up_h
        act[0, k, d] = (gate_h * jax.nn.sigmoid(gate_h) * up_h).astype(jnp.bfloat16)
        for p in range(1, GROUPS):
            ag1(k, p).start()
        await_slabs(sy, ry, sy_s, sy_r, k, 1)
        for h in range(2):
            ys[k, :, h * half : (h + 1) * half] = from_slabs(ry, k, h)
        partial_sums(k, 2, lax.dot_general(ys[k], wd[...], NT, preferred_element_type=jnp.float32))
        for p in range(1, GROUPS):
            rs2(k, p).start()
        return carry

    lax.fori_loop(0, CHUNKS, second, 0)

    def whole(q, k):
        return act[q, k].reshape(ROWS, act.shape[4])

    def third(k, carry):
        for p in range(1, GROUPS):
            rs2(k, p).wait()
        d_h = reduced(k, 2)
        gate_h, up_h = gu[k, 0], gu[k, 1]
        sigma = jax.nn.sigmoid(gate_h)
        act[1, k, d] = (d_h * up_h * sigma * (1.0 + gate_h * (1.0 - sigma))).astype(jnp.bfloat16)
        act[2, k, d] = (d_h * (gate_h * sigma)).astype(jnp.bfloat16)
        for p in range(1, GROUPS):
            ag2(k, p).start()
        for p in range(1, GROUPS):
            ag1(k, p).wait()
        y = dot(whole(0, k), wd[...])
        await_sent(sx, rx, sx_s, sx_r, k, 1)
        to_slabs(sx, k, y)
        send_slabs(sx, by, bks_y, bkr_y, k, -1)
        return carry

    lax.fori_loop(0, CHUNKS, third, 0)

    def fourth(k, carry):
        for p in range(1, GROUPS):
            ag2(k, p).wait()
        dx = lax.dot_general(whole(1, k), wg[...], NT, preferred_element_type=jnp.float32)
        dx += lax.dot_general(whole(2, k), wu[...], NT, preferred_element_type=jnp.float32)
        await_sent(sy, ry, sy_s, sy_r, k, 1)
        to_slabs(sy, k, dx)
        send_slabs(sy, bx, bks_x, bkr_x, k, -1)
        return carry

    lax.fori_loop(0, CHUNKS, fourth, 0)

    block = 256

    def all_rows(q):
        return act[q].reshape(CHUNKS * ROWS, act.shape[4])

    def weight_grads(b, carry):
        cols = pl.ds(pl.multiple_of(b * block, block), block)
        x = xs[:, :, cols].reshape(CHUNKS * ROWS, block)
        gg[0, cols, :] = lax.dot_general(x, all_rows(1), TN, preferred_element_type=jnp.float32).astype(jnp.bfloat16)
        gg[1, cols, :] = lax.dot_general(x, all_rows(2), TN, preferred_element_type=jnp.float32).astype(jnp.bfloat16)
        return carry

    lax.fori_loop(0, width // block, weight_grads, 0)
    outs = [
        pltpu.make_async_copy(gg.at[0], g_gate.at[0], loc.at[2]),
        pltpu.make_async_copy(gg.at[1], g_up.at[0], loc.at[3]),
        pltpu.make_async_copy(wd, g_down.at[0], loc.at[4]),
    ]
    outs[0].start()
    outs[1].start()

    def down_grads(b, carry):
        cols = pl.ds(pl.multiple_of(b * block, block), block)
        dy = ys[:, :, cols].reshape(CHUNKS * ROWS, block)
        wd[:, cols] = lax.dot_general(all_rows(0), dy, TN, preferred_element_type=jnp.float32).astype(jnp.bfloat16)
        return carry

    lax.fori_loop(0, width // block, down_grads, 0)
    outs[2].start()

    def final(src, dst, s, r, p):
        q = lax.rem(d + p, GROUPS)
        own = dst.at[:, pl.ds(pl.multiple_of(d * width, width), width)]
        return remote(src.at[q], own, s.at[p - 1], r.at[p - 1], ring(p))

    def combine(buf, matrix, stage):
        for h in range(2):
            total = jnp.zeros((GROUPS * TOK, half), jnp.float32)
            for k in range(CHUNKS):
                total += lax.dot_general(matrix(k), from_slabs(buf, k, h), TN, preferred_element_type=jnp.float32)
            stage[:, :, h * half : (h + 1) * half] = total.astype(jnp.bfloat16).reshape(GROUPS, TOK, half)

    def own_out(src, dst, sem):
        return pltpu.make_async_copy(src.at[d], dst.at[:, columns(0)], sem)

    def back_y(k, carry):
        await_slabs(sx, by, bks_y, bkr_y, k, -1)
        await_sent(sx, by, bks_y, bkr_y, k, -1)
        return carry

    lax.fori_loop(0, CHUNKS, back_y, 0)
    combine(by, lambda k: og[k].astype(jnp.bfloat16), tx)
    for p in range(1, GROUPS):
        final(tx, mixed, fm_s, fm_r, p).start()
    own_out(tx, mixed, loc.at[0]).start()

    def back_x(k, carry):
        await_slabs(sy, bx, bks_x, bkr_x, k, -1)
        await_sent(sy, bx, bks_x, bkr_x, k, -1)
        return carry

    lax.fori_loop(0, CHUNKS, back_x, 0)
    combine(bx, lambda k: oh[k], tc)
    for p in range(1, GROUPS):
        final(tc, d_tokens, fd_s, fd_r, p).start()
    own_out(tc, d_tokens, loc.at[1]).start()
    for p in range(1, GROUPS):
        final(tx, mixed, fm_s, fm_r, p).wait()
        final(tc, d_tokens, fd_s, fd_r, p).wait()
    own_out(tx, mixed, loc.at[0]).wait()
    own_out(tc, d_tokens, loc.at[1]).wait()
    for o in outs:
        o.wait()


def shards(tokens, routes, gates, cotangent, w_gate, w_up, w_down):
    tok, full = tokens.shape
    ff = w_gate.shape[2]
    width = full // GROUPS
    bf16, f32 = jnp.bfloat16, jnp.float32
    tab = jnp.concatenate([routes.astype(f32), gates], axis=1).T
    hbm = pl.BlockSpec(memory_space=pl.ANY)
    vmem = pl.BlockSpec(memory_space=pltpu.VMEM)
    slabs = pltpu.VMEM((EXPERTS, 2 * SLAB, width // 2), bf16)
    sem = pltpu.SemaphoreType.DMA
    return pl.pallas_call(
        kernel,
        out_shape=(
            jax.ShapeDtypeStruct(tokens.shape, bf16),
            jax.ShapeDtypeStruct(tokens.shape, bf16),
            jax.ShapeDtypeStruct(w_gate.shape, bf16),
            jax.ShapeDtypeStruct(w_up.shape, bf16),
            jax.ShapeDtypeStruct(w_down.shape, bf16),
        ),
        in_specs=[vmem] + [hbm] * 5,
        out_specs=(hbm,) * 5,
        scratch_shapes=[
            pltpu.VMEM((GROUPS, 8, tok), f32),
            pltpu.VMEM((GROUPS, tok, width), bf16),
            pltpu.VMEM((GROUPS, tok, width), bf16),
            pltpu.VMEM((CHUNKS, ROWS, GROUPS * tok), bf16),
            pltpu.VMEM((CHUNKS, ROWS, GROUPS * tok), f32),
            pltpu.VMEM((width, ff), bf16),
            pltpu.VMEM((width, ff), bf16),
            pltpu.VMEM((ff, width), bf16),
            slabs, slabs, slabs, slabs, slabs, slabs,
            pltpu.VMEM((CHUNKS, ROWS, width), bf16),
            pltpu.VMEM((CHUNKS, ROWS, width), bf16),
            pltpu.VMEM((CHUNKS, GROUPS, 3, OWN, ff), bf16),
            pltpu.VMEM((CHUNKS, GROUPS - 1, 3, OWN, ff), bf16),
            pltpu.VMEM((3, CHUNKS, GROUPS, OWN, ff), bf16),
            pltpu.VMEM((CHUNKS, 2, OWN, ff), f32),
            pltpu.VMEM((2, width, ff), bf16),
            sem((3,)), sem((3,)), sem((3,)), sem((3,)), sem((3,)), sem((3,)), sem((5,)),
        ]
        + [sem((EXPERTS,))] * 8
        + [sem((CHUNKS, 3))] * 8
        + [sem((3,))] * 4,
        compiler_params=pltpu.CompilerParams(
            collective_id=0, has_side_effects=True, vmem_limit_bytes=62 * 2**20
        ),
        cost_estimate=pl.CostEstimate(flops=24 * 10**9, bytes_accessed=14 * 10**6, transcendentals=500000),
    )(tab, tokens, cotangent, w_gate, w_up, w_down)


def solution(mesh):
    placed = (
        P(("dp", "tensor", "context"), None),
        P(("dp", "tensor", "context"), None),
        P(("dp", "tensor", "context"), None),
        P(("dp", "tensor", "context"), None),
        P(("tensor", "context"), "dp", None),
        P(("tensor", "context"), "dp", None),
        P(("tensor", "context"), None, "dp"),
    )
    return jax.shard_map(
        shards,
        mesh=mesh,
        in_specs=placed,
        out_specs=(
            P(("dp", "tensor", "context"), None),
            P(("dp", "tensor", "context"), None),
            P(("tensor", "context"), "dp", None),
            P(("tensor", "context"), "dp", None),
            P(("tensor", "context"), None, "dp"),
        ),
        check_vma=False,
    )
```

time: 439 us -> 232 us (0.53)
  waiting for transfers between devices: 251 us -> 0 us
  Pallas kernels: 0 us -> 218 us
  matrix products: 55 us -> 0 us
  local copies, waits for them, and re-layouts: 51.1 us -> 9.26 us
  starting transfers between devices: 33.3 us -> 0 us
  other arithmetic: 28.4 us -> 1.94 us
  between operations: 14.6 us -> 0.65 us
    pallas_call x0 -> x1, Pallas kernels: none -> 218 us  [shards(): pl.pallas_call(kernel, out_shape=(jax.ShapeDtypeStruct(tokens.shape, bf16...]
    all_to_all x4 -> x0, waiting for transfers between devices: 176 us -> none  [route(): lax.all_to_all(shaped, ('tensor', 'context'), split_axis=0, concat_axis=0...]
    all_gather x3 -> x0, waiting for transfers between devices: 58.5 us -> none  [the longest x1 58.5 us: shards(): lax.all_gather(wg, 'dp', axis=0, tiled=True)]
    dot_general x9 -> x0, matrix products: 55 us -> none  [the longest x1 7.87 us: expert_pass(): g_up = jnp.dot(x_rows.T, d_up, preferred_element_type=jnp.float32)]
    all_to_all x4 -> x0, starting transfers between devices: 32.5 us -> none  [route(): lax.all_to_all(shaped, ('tensor', 'context'), split_axis=0, concat_axis=0...]
    reshape x10 -> x0, local copies, waits for them, and re-layouts: 29.7 us -> none  [the longest x4 14.9 us: route(): return moved.reshape(experts * cap, depth)]
    reduce_sum x5 -> x0, other arithmetic: 17.3 us -> none  [the longest x1 9.64 us: shards(): mixed = jnp.sum(gates[:, :, None] * y_taken, axis=1).astype(jnp.bfloat16)]
    gather x4 -> x0, local copies, waits for them, and re-layouts: 14.1 us -> none  [the longest x1 3.87 us: shards(): picked = jnp.take(tokens, owner, axis=0)]
  transfers between devices with their start and end apart: 10 -> 0, of which waited for: 6 -> 0; matrix products, arithmetic and copies ran while one was open for 28% -> 0% of each run, Pallas kernels for 0% -> 0%
where the time goes in v1:
time: 232 us; the launch traced here: 229 us
  Pallas kernels  218 us (94%)
  local copies, waits for them, and re-layouts  9.26 us (4%)
    pallas_call x1, Pallas kernels, shards(): pl.pallas_call(kernel, out_shape=(jax.ShapeDtypeStruct(tokens.shape, bf16...  218 us
    unnamed x13, local copies, waits for them, and re-layouts  9.26 us

profile of v1, /device:TPU:1, one launch (start us, length us, event | category | flops | bytes accessed | tf_op | source)
XLA Modules:
  0.0 229.4 jit_solution(12223641829884478043)
XLA Ops:
  0.6 0.7 convert_element_type.3
  1.3 1.3 maximum_bitcast_fusion.tab_ref
  2.6 217.5 %shard_map.110 = (bf16[128,4096]{1,0:T(8,128)(2,1)}, bf16[128,4096]{1,0:T(8,128)(2,1)}, bf16[1,1024,768]{2,1,0:T(8,128)(2,1)}, bf16[1,1024,768]{2,1,0:T(8,128)(2,1)}, bf16[1,768,1024]{2,1,0:T(8,128)(2,1)}) custom-call(f32[4,128]{1,0:T(4,128)} %maximum_bitcast_fusion.tab_ref, bf16[128,4096]{1,0:T(8,128)(2,1)} %tokens.1, bf16[128,4096]{1,0:T(8,128)(2,1)} %cotangent.1, ...), custom_call_target="tpu_custom_call" | custom-call | flops 24000000000 | bytes 14000000 | tf_op jit(solution)/shard_map/pallas_call | solution.py:385
  220.1 0.0 copy-start.3
  220.1 2.4 %copy.17 = bf16[128,4096]{1,0:T(8,128)(2,1)} copy(bf16[128,4096]{1,0:T(8,128)(2,1)} %get-tuple-element.10) | data formatting | bytes 2097152
  222.5 0.0 copy-done.3
  222.5 0.0 copy-start.2
  222.5 1.0 copy.18
  223.5 0.8 copy-done.2
  224.3 0.0 copy-start.1
  224.3 1.1 copy.19
  225.4 0.8 copy-done.1
  226.3 0.0 copy-start
  226.3 1.1 copy.20
  227.4 0.8 copy-done
  228.2 1.1 copy.21
Async XLA Ops:
  220.1 2.4 %copy-start.3 = (bf16[128,4096]{1,0:T(8,128)(2,1)S(1)}, bf16[128,4096]{1,0:T(8,128)(2,1)}, u32[]{:S(2)}) copy-start(bf16[128,4096]{1,0:T(8,128)(2,1)} %get-tuple-element.11) | copy-start | bytes 3145732
  222.5 1.8 copy-start.2
  224.3 2.0 copy-start.1
  226.3 2.0 copy-start

commit v2 on v1

--- a/solution.py
+++ b/solution.py
@@ -8,6 +8,9 @@
 from jax.sharding import PartitionSpec as P
 
 MESH = pl.DeviceIdType.MESH
+BACKY_FIRST = True
+DY_AT = 1
+Y_EARLY = True
 GROUPS = 4
 EXPERTS = 32
 CAP = 10
@@ -30,10 +33,10 @@
 def kernel(
     tab_ref, tokens, cotangent, w_gate, w_up, w_down,
     mixed, d_tokens, g_gate, g_up, g_down,
-    tb, tx, tc, oh, og, wg, wu, wd, sx, sy, rx, ry, by, bx, xs, ys, part, got, act, gu, gg,
+    tb, tx, tc, oh, og, wg, wu, wd, sx, sy, rx, ry, by, bx, xs, ys, part, got, relay, act, gu, gg,
     tab_s, tab_r, tx_s, tx_r, tc_s, tc_r, loc,
     sx_s, sx_r, sy_s, sy_r, bks_y, bkr_y, bks_x, bkr_x,
-    rs1_s, rs1_r, rs2_s, rs2_r, ag1_s, ag1_r, ag2_s, ag2_r,
+    rs_s, rs_r, ag_s, ag_r,
     fm_s, fm_r, fd_s, fd_r,
 ):
     d = lax.axis_index("dp")
@@ -78,30 +81,6 @@
     lax.fori_loop(0, EXPERTS, greet, 0)
     for p in range(1, GROUPS):
         pl.semaphore_signal(barrier, inc=1, device_id=ring(p), device_id_type=MESH)
-    pl.semaphore_wait(barrier, EXPERTS - 1 + GROUPS - 1)
-
-    def columns(p):
-        q = lax.rem(d + p, GROUPS)
-        return pl.ds(pl.multiple_of(q * width, width), width)
-
-    def dense(src, dst, s, r, p):
-        return remote(src.at[:, columns(p)], dst.at[d], s.at[p - 1], r.at[p - 1], ring(p))
-
-    own_tx = pltpu.make_async_copy(tokens.at[:, columns(0)], tx.at[d], loc.at[0])
-    own_tc = pltpu.make_async_copy(cotangent.at[:, columns(0)], tc.at[d], loc.at[1])
-    for p in range(1, GROUPS):
-        dense(tokens, tx, tx_s, tx_r, p).start()
-    own_tx.start()
-    for p in range(1, GROUPS):
-        dense(cotangent, tc, tc_s, tc_r, p).start()
-    own_tc.start()
-    weights = [
-        pltpu.make_async_copy(w_gate.at[0], wg, loc.at[2]),
-        pltpu.make_async_copy(w_up.at[0], wu, loc.at[3]),
-        pltpu.make_async_copy(w_down.at[0], wd, loc.at[4]),
-    ]
-    for w in weights:
-        w.start()
 
     e = lax.broadcasted_iota(jnp.int32, (EXPERTS, TOK), 0)
     e_core = (e >> 3) & 1
@@ -126,11 +105,37 @@
     key1 = jnp.sum(chosen1 * place, axis=0, keepdims=True)
     tb[d] = jnp.concatenate([key0, key1, tab[2:4, :], jnp.zeros((4, TOK), jnp.float32)], axis=0)
 
+    pl.semaphore_wait(barrier, EXPERTS - 1 + GROUPS - 1)
+
     def tables(p):
         return remote(tb.at[d], tb.at[d], tab_s.at[p - 1], tab_r.at[p - 1], ring(p))
 
     for p in range(1, GROUPS):
         tables(p).start()
+
+    def columns(p):
+        q = lax.rem(d + p, GROUPS)
+        return pl.ds(pl.multiple_of(q * width, width), width)
+
+    def dense(src, dst, s, r, p):
+        return remote(src.at[:, columns(p)], dst.at[d], s.at[p - 1], r.at[p - 1], ring(p))
+
+    own_tx = pltpu.make_async_copy(tokens.at[:, columns(0)], tx.at[d], loc.at[0])
+    own_tc = pltpu.make_async_copy(cotangent.at[:, columns(0)], tc.at[d], loc.at[1])
+    for p in range(1, GROUPS):
+        dense(tokens, tx, tx_s, tx_r, p).start()
+    own_tx.start()
+    for p in range(1, GROUPS):
+        dense(cotangent, tc, tc_s, tc_r, p).start()
+    own_tc.start()
+    weights = [
+        pltpu.make_async_copy(w_gate.at[0], wg, loc.at[2]),
+        pltpu.make_async_copy(w_up.at[0], wu, loc.at[3]),
+        pltpu.make_async_copy(w_down.at[0], wd, loc.at[4]),
+    ]
+    for w in weights:
+        w.start()
+
     for p in range(1, GROUPS):
         tables(p).wait()
 
@@ -146,7 +151,7 @@
         return v.reshape(ROWS, half).astype(jnp.bfloat16)
 
     def slab_copy(src, dst, s, r, j, sign):
-        return remote(src.at[j], dst.at[j], s.at[j], r.at[j], peer(j, sign))
+        return remote(src.at[j], dst.at[j], s.at[j // PER], r.at[j // PER], peer(j, sign))
 
     def each_slot(k, act_on):
         def body(i, carry):
@@ -167,11 +172,22 @@
         def _():
             dst[SELF] = src[SELF]
 
+    def await_bytes(buf, sem, k):
+        @pl.when(k == SELF // PER)
+        def _():
+            ref = buf.at[pl.ds(SELF + 1, PER - 1)]
+            pltpu.make_async_copy(ref, ref, sem.at[k]).wait()
+
+        @pl.when(k != SELF // PER)
+        def _():
+            ref = buf.at[pl.ds(k * PER, PER)]
+            pltpu.make_async_copy(ref, ref, sem.at[k]).wait()
+
     def await_slabs(src, dst, s, r, k, sign):
-        each_slot(k, lambda j: slab_copy(src, dst, s, r, j, sign).wait_recv())
+        await_bytes(dst, r, k)
 
     def await_sent(src, dst, s, r, k, sign):
-        each_slot(k, lambda j: slab_copy(src, dst, s, r, j, sign).wait_send())
+        await_bytes(src, s, k)
 
     for p in range(1, GROUPS):
         dense(tokens, tx, tx_s, tx_r, p).wait()
@@ -191,111 +207,201 @@
 
     lax.fori_loop(0, CHUNKS, send_x, 0)
 
-    for p in range(1, GROUPS):
-        dense(cotangent, tc, tc_s, tc_r, p).wait()
-    own_tc.wait()
-
     def send_dy(k, carry):
         weight = jnp.sum(og[k], axis=1, keepdims=True)
         to_slabs(sy, k, dot(oh[k], tc[...].reshape(GROUPS * TOK, width)) * weight)
         send_slabs(sy, ry, sy_s, sy_r, k, 1)
         return carry
 
-    lax.fori_loop(0, CHUNKS, send_dy, 0)
+    def await_cot():
+        for p in range(1, GROUPS):
+            dense(cotangent, tc, tc_s, tc_r, p).wait()
+        own_tc.wait()
+
+    if DY_AT < 0:
+        await_cot()
+        lax.fori_loop(0, CHUNKS, send_dy, 0)
     for w in weights:
         w.wait()
 
-    def rs1(k, p):
-        q = lax.rem(d + p, GROUPS)
-        return remote(
-            part.at[k, q, pl.ds(0, 2)], got.at[k, p - 1, pl.ds(0, 2)], rs1_s.at[k, p - 1], rs1_r.at[k, p - 1], ring(p)
-        )
-
-    def rs2(k, p):
-        q = lax.rem(d + p, GROUPS)
-        return remote(part.at[k, q, 2], got.at[k, p - 1, 2], rs2_s.at[k, p - 1], rs2_r.at[k, p - 1], ring(p))
-
-    def ag1(k, p):
-        return remote(act.at[0, k, d], act.at[0, k, d], ag1_s.at[k, p - 1], ag1_r.at[k, p - 1], ring(p))
-
-    def ag2(k, p):
-        own = act.at[pl.ds(1, 2), k, d]
-        return remote(own, own, ag2_s.at[k, p - 1], ag2_r.at[k, p - 1], ring(p))
+    def way(k, q, mixed_q):
+        if q == mixed_q:
+            return 1 + 2 * lax.rem(k, 2)
+        return 1 if q == min({0, 1, 2} - {mixed_q}) else 3
+
+    def towards(n):
+        return lax.rem(d + n, GROUPS)
+
+    def rs(k, q, kind):
+        w = way(k, q, 2)
+        s, r = rs_s.at[0], rs_r.at[k, q, min(kind, 1)]
+        if kind == 0:
+            return remote(part.at[k, towards(2), q], relay.at[k, q], s, r, ring(w))
+        if kind == 1:
+            return remote(part.at[k, towards(4 - w), q], got.at[k, q, 0], s, r, ring(4 - w))
+        return remote(part.at[k, towards(w), q], got.at[k, q, 1], s, r, ring(w))
+
+    def rs_start(k, q):
+        rs(k, q, 0).start()
+        rs(k, q, 1).start()
+
+    def rs_add(k, q):
+        rs(k, q, 0).wait_recv()
+        o = towards(way(k, q, 2))
+        part[k, o, q] = (part[k, o, q].astype(jnp.float32) + relay[k, q].astype(jnp.float32)).astype(jnp.bfloat16)
+        rs(k, q, 2).start()
+
+    def rs_total(k, q):
+        pltpu.make_async_copy(got.at[k, q], got.at[k, q], rs_r.at[k, q, 1]).wait()
+        total = part[k, d, q].astype(jnp.float32)
+        return total + got[k, q, 0].astype(jnp.float32) + got[k, q, 1].astype(jnp.float32)
+
+    def ag(k, q, kind):
+        w = way(k, q, 0)
+        s, r = ag_s.at[0], ag_r.at[k, q, min(kind, 1)]
+        o = d if kind < 2 else towards(4 - w)
+        return remote(act.at[q, k, o], act.at[q, k, o], s, r, ring(w if kind != 1 else 4 - w))
+
+    def ag_start(k, q):
+        ag(k, q, 0).start()
+        ag(k, q, 1).start()
+
+    def ag_forward(k, q):
+        ag(k, q, 0).wait_recv()
+        ag(k, q, 2).start()
+
+    def ag_whole(k, q):
+        two = act.at[q, k, pl.ds(0, 2)]
+        pltpu.make_async_copy(two, two, ag_r.at[k, q, 1]).wait()
+        return act[q, k].reshape(ROWS, act.shape[4])
 
     def partial_sums(k, q, value):
         part[k, :, q] = value.astype(jnp.bfloat16).reshape(GROUPS, OWN, value.shape[1])
 
-    def first(k, carry):
+    def in_turn(step, later):
+        def body(k, carry):
+            step(k)
+
+            @pl.when(k > 0)
+            def _():
+                later(k - 1)
+
+            return carry
+
+        lax.fori_loop(0, CHUNKS, body, 0)
+        later(CHUNKS - 1)
+
+    def first(k):
         await_slabs(sx, rx, sx_s, sx_r, k, 1)
         for h in range(2):
             xs[k, :, h * half : (h + 1) * half] = from_slabs(rx, k, h)
         partial_sums(k, 0, dot(xs[k], wg[...]))
+        rs_start(k, 0)
         partial_sums(k, 1, dot(xs[k], wu[...]))
-        for p in range(1, GROUPS):
-            rs1(k, p).start()
-        return carry
-
-    lax.fori_loop(0, CHUNKS, first, 0)
-
-    def reduced(k, q):
-        total = part[k, d, q].astype(jnp.float32)
-        for p in range(1, GROUPS):
-            total += got[k, p - 1, q].astype(jnp.float32)
-        return total
-
-    def second(k, carry):
-        for p in range(1, GROUPS):
-            rs1(k, p).wait()
-        gate_h, up_h = reduced(k, 0), reduced(k, 1)
+        rs_start(k, 1)
+        if DY_AT >= 0:
+            @pl.when(k == DY_AT)
+            def _():
+                await_cot()
+
+            @pl.when(k >= DY_AT)
+            def _():
+                send_dy(k - DY_AT, 0)
+
+    def first_later(k):
+        rs_add(k, 0)
+        rs_add(k, 1)
+
+    in_turn(first, first_later)
+    if DY_AT > 0:
+        lax.fori_loop(CHUNKS - DY_AT, CHUNKS, send_dy, 0)
+
+    def send_y(k):
+        y = dot(ag_whole(k, 0), wd[...])
+        await_sent(sx, rx, sx_s, sx_r, k, 1)
+        to_slabs(sx, k, y)
+        send_slabs(sx, by, bks_y, bkr_y, k, -1)
+
+    def second(k):
+        gate_h, up_h = rs_total(k, 0), rs_total(k, 1)
         gu[k, 0] = gate_h
         gu[k, 1] = up_h
         act[0, k, d] = (gate_h * jax.nn.sigmoid(gate_h) * up_h).astype(jnp.bfloat16)
-        for p in range(1, GROUPS):
-            ag1(k, p).start()
+        ag_start(k, 0)
         await_slabs(sy, ry, sy_s, sy_r, k, 1)
         for h in range(2):
             ys[k, :, h * half : (h + 1) * half] = from_slabs(ry, k, h)
         partial_sums(k, 2, lax.dot_general(ys[k], wd[...], NT, preferred_element_type=jnp.float32))
-        for p in range(1, GROUPS):
-            rs2(k, p).start()
-        return carry
-
-    lax.fori_loop(0, CHUNKS, second, 0)
-
-    def whole(q, k):
-        return act[q, k].reshape(ROWS, act.shape[4])
-
-    def third(k, carry):
-        for p in range(1, GROUPS):
-            rs2(k, p).wait()
-        d_h = reduced(k, 2)
+        rs_start(k, 2)
+
+    def second_later(k):
+        ag_forward(k, 0)
+        rs_add(k, 2)
+        if Y_EARLY:
+            @pl.when(k > 0)
+            def _():
+                send_y(k - 1)
+
+    in_turn(second, second_later)
+    if Y_EARLY:
+        send_y(CHUNKS - 1)
+
+    def third(k):
+        d_h = rs_total(k, 2)
         gate_h, up_h = gu[k, 0], gu[k, 1]
         sigma = jax.nn.sigmoid(gate_h)
         act[1, k, d] = (d_h * up_h * sigma * (1.0 + gate_h * (1.0 - sigma))).astype(jnp.bfloat16)
+        ag_start(k, 1)
         act[2, k, d] = (d_h * (gate_h * sigma)).astype(jnp.bfloat16)
-        for p in range(1, GROUPS):
-            ag2(k, p).start()
-        for p in range(1, GROUPS):
-            ag1(k, p).wait()
-        y = dot(whole(0, k), wd[...])
-        await_sent(sx, rx, sx_s, sx_r, k, 1)
-        to_slabs(sx, k, y)
-        send_slabs(sx, by, bks_y, bkr_y, k, -1)
-        return carry
-
-    lax.fori_loop(0, CHUNKS, third, 0)
+        ag_start(k, 2)
+        if not Y_EARLY:
+            send_y(k)
+
+    def third_later(k):
+        ag_forward(k, 1)
+        ag_forward(k, 2)
+
+    in_turn(third, third_later)
 
     def fourth(k, carry):
-        for p in range(1, GROUPS):
-            ag2(k, p).wait()
-        dx = lax.dot_general(whole(1, k), wg[...], NT, preferred_element_type=jnp.float32)
-        dx += lax.dot_general(whole(2, k), wu[...], NT, preferred_element_type=jnp.float32)
+        dx = lax.dot_general(ag_whole(k, 1), wg[...], NT, preferred_element_type=jnp.float32)
+        dx += lax.dot_general(ag_whole(k, 2), wu[...], NT, preferred_element_type=jnp.float32)
         await_sent(sy, ry, sy_s, sy_r, k, 1)
         to_slabs(sy, k, dx)
         send_slabs(sy, bx, bks_x, bkr_x, k, -1)
         return carry
 
     lax.fori_loop(0, CHUNKS, fourth, 0)
+
+    def final(src, dst, s, r, p):
+        q = lax.rem(d + p, GROUPS)
+        own = dst.at[:, pl.ds(pl.multiple_of(d * width, width), width)]
+        return remote(src.at[q], own, s.at[p - 1], r.at[p - 1], ring(p))
+
+    def combine(buf, matrix, stage):
+        for h in range(2):
+            total = jnp.zeros((GROUPS * TOK, half), jnp.float32)
+            for k in range(CHUNKS):
+                total += lax.dot_general(matrix(k), from_slabs(buf, k, h), TN, preferred_element_type=jnp.float32)
+            stage[:, :, h * half : (h + 1) * half] = total.astype(jnp.bfloat16).reshape(GROUPS, TOK, half)
+
+    def own_out(src, dst, sem):
+        return pltpu.make_async_copy(src.at[d], dst.at[:, columns(0)], sem)
+
+    def finish_y():
+        def back_y(k, carry):
+            await_slabs(sx, by, bks_y, bkr_y, k, -1)
+            await_sent(sx, by, bks_y, bkr_y, k, -1)
+            return carry
+
+        lax.fori_loop(0, CHUNKS, back_y, 0)
+        combine(by, lambda k: og[k].astype(jnp.bfloat16), tx)
+        for p in range(1, GROUPS):
+            final(tx, mixed, fm_s, fm_r, p).start()
+        own_out(tx, mixed, loc.at[0]).start()
+
+    if BACKY_FIRST:
+        finish_y()
 
     block = 256
 
@@ -327,31 +433,8 @@
     lax.fori_loop(0, width // block, down_grads, 0)
     outs[2].start()
 
-    def final(src, dst, s, r, p):
-        q = lax.rem(d + p, GROUPS)
-        own = dst.at[:, pl.ds(pl.multiple_of(d * width, width), width)]
-        return remote(src.at[q], own, s.at[p - 1], r.at[p - 1], ring(p))
-
-    def combine(buf, matrix, stage):
-        for h in range(2):
-            total = jnp.zeros((GROUPS * TOK, half), jnp.float32)
-            for k in range(CHUNKS):
-                total += lax.dot_general(matrix(k), from_slabs(buf, k, h), TN, preferred_element_type=jnp.float32)
-            stage[:, :, h * half : (h + 1) * half] = total.astype(jnp.bfloat16).reshape(GROUPS, TOK, half)
-
-    def own_out(src, dst, sem):
-        return pltpu.make_async_copy(src.at[d], dst.at[:, columns(0)], sem)
-
-    def back_y(k, carry):
-        await_slabs(sx, by, bks_y, bkr_y, k, -1)
-        await_sent(sx, by, bks_y, bkr_y, k, -1)
-        return carry
-
-    lax.fori_loop(0, CHUNKS, back_y, 0)
-    combine(by, lambda k: og[k].astype(jnp.bfloat16), tx)
-    for p in range(1, GROUPS):
-        final(tx, mixed, fm_s, fm_r, p).start()
-    own_out(tx, mixed, loc.at[0]).start()
+    if not BACKY_FIRST:
+        finish_y()
 
     def back_x(k, carry):
         await_slabs(sy, bx, bks_x, bkr_x, k, -1)
@@ -370,6 +453,14 @@
     own_out(tc, d_tokens, loc.at[1]).wait()
     for o in outs:
         o.wait()
+    sums, gathers = part.at[pl.ds(0, 3)], act.at[:, pl.ds(0, 3)]
+    pltpu.make_async_copy(sums, sums, rs_s.at[0]).wait()
+    pltpu.make_async_copy(gathers, gathers, ag_s.at[0]).wait()
+
+
+def publish(*refs):
+    for i in range(5):
+        refs[5 + i][...] = refs[i][...]
 
 
 def shards(tokens, routes, gates, cotangent, w_gate, w_up, w_down):
@@ -382,7 +473,7 @@
     vmem = pl.BlockSpec(memory_space=pltpu.VMEM)
     slabs = pltpu.VMEM((EXPERTS, 2 * SLAB, width // 2), bf16)
     sem = pltpu.SemaphoreType.DMA
-    return pl.pallas_call(
+    results = pl.pallas_call(
         kernel,
         out_shape=(
             jax.ShapeDtypeStruct(tokens.shape, bf16),
@@ -406,20 +497,35 @@
             pltpu.VMEM((CHUNKS, ROWS, width), bf16),
             pltpu.VMEM((CHUNKS, ROWS, width), bf16),
             pltpu.VMEM((CHUNKS, GROUPS, 3, OWN, ff), bf16),
-            pltpu.VMEM((CHUNKS, GROUPS - 1, 3, OWN, ff), bf16),
+            pltpu.VMEM((CHUNKS, 3, 2, OWN, ff), bf16),
+            pltpu.VMEM((CHUNKS, 3, OWN, ff), bf16),
             pltpu.VMEM((3, CHUNKS, GROUPS, OWN, ff), bf16),
             pltpu.VMEM((CHUNKS, 2, OWN, ff), f32),
             pltpu.VMEM((2, width, ff), bf16),
             sem((3,)), sem((3,)), sem((3,)), sem((3,)), sem((3,)), sem((3,)), sem((5,)),
         ]
-        + [sem((EXPERTS,))] * 8
-        + [sem((CHUNKS, 3))] * 8
+        + [sem((CHUNKS,))] * 8
+        + [sem((1,)), sem((CHUNKS, 3, 2)), sem((1,)), sem((CHUNKS, 3, 2))]
         + [sem((3,))] * 4,
         compiler_params=pltpu.CompilerParams(
             collective_id=0, has_side_effects=True, vmem_limit_bytes=62 * 2**20
         ),
         cost_estimate=pl.CostEstimate(flops=24 * 10**9, bytes_accessed=14 * 10**6, transcendentals=500000),
     )(tab, tokens, cotangent, w_gate, w_up, w_down)
+    specs = [
+        pl.BlockSpec((16, 4096), lambda i: (i, 0)),
+        pl.BlockSpec((16, 4096), lambda i: (i, 0)),
+        pl.BlockSpec((1, 128, 768), lambda i: (0, i, 0)),
+        pl.BlockSpec((1, 128, 768), lambda i: (0, i, 0)),
+        pl.BlockSpec((1, 96, 1024), lambda i: (0, i, 0)),
+    ]
+    return pl.pallas_call(
+        publish,
+        out_shape=[jax.ShapeDtypeStruct(r.shape, r.dtype) for r in results],
+        grid=(8,),
+        in_specs=specs,
+        out_specs=specs,
+    )(*results)
 
 
 def solution(mesh):

time: 232 us -> 198 us (0.85)
  Pallas kernels: 218 us -> 195 us
  local copies, waits for them, and re-layouts: 9.26 us -> 0 us
    pallas_call x1, Pallas kernels: 218 us -> 187 us  [shards(): pl.pallas_call(kernel, out_shape=(jax.ShapeDtypeStruct(tokens.shape, bf16...]
    unnamed x13 -> x0, local copies, waits for them, and re-layouts: 9.26 us -> none
    pallas_call x0 -> x1, Pallas kernels: none -> 8.05 us  [shards(): pl.pallas_call(publish, out_shape=[jax.ShapeDtypeStruct(r.shape, r.dtype)...]
where the time goes in v2:
time: 198 us; the launch traced here: 197 us
  Pallas kernels  195 us (98%)
    pallas_call x1, Pallas kernels, shards(): pl.pallas_call(kernel, out_shape=(jax.ShapeDtypeStruct(tokens.shape, bf16...  187 us
    pallas_call x1, Pallas kernels, shards(): pl.pallas_call(publish, out_shape=[jax.ShapeDtypeStruct(r.shape, r.dtype)...  8.05 us

profile of v2, /device:TPU:1, one launch (start us, length us, event | category | flops | bytes accessed | tf_op | source)
XLA Modules:
  0.0 197.5 jit_solution(10346823335502580903)
XLA Ops:
  0.6 0.7 convert_element_type.3
  1.3 1.3 maximum_bitcast_fusion.tab_ref
  2.6 186.9 %shard_map.110 = (bf16[128,4096]{1,0:T(8,128)(2,1)}, bf16[128,4096]{1,0:T(8,128)(2,1)}, bf16[1,1024,768]{2,1,0:T(8,128)(2,1)}, bf16[1,1024,768]{2,1,0:T(8,128)(2,1)}, bf16[1,768,1024]{2,1,0:T(8,128)(2,1)}) custom-call(f32[4,128]{1,0:T(4,128)} %maximum_bitcast_fusion.tab_ref, bf16[128,4096]{1,0:T(8,128)(2,1)} %tokens.1, bf16[128,4096]{1,0:T(8,128)(2,1)} %cotangent.1, ...), custom_call_target="tpu_custom_call" | custom-call | flops 24000000000 | bytes 14000000 | tf_op jit(solution)/shard_map/pallas_call | solution.py:476
  189.4 8.1 %shard_map.111 = (bf16[128,4096]{1,0:T(8,128)(2,1)}, bf16[128,4096]{1,0:T(8,128)(2,1)}, bf16[1,1024,768]{2,1,0:T(8,128)(2,1)}, bf16[1,1024,768]{2,1,0:T(8,128)(2,1)}, bf16[1,768,1024]{2,1,0:T(8,128)(2,1)}) custom-call(bf16[128,4096]{1,0:T(8,128)(2,1)} %get-tuple-element.10.refs_0_, bf16[128,4096]{1,0:T(8,128)(2,1)} %get-tuple-element.11.refs_1_, ...), custom_call_target="tpu_custom_call" | custom-call | tf_op jit(solution)/shard_map/pallas_call | solution.py:522

commit v3 on v2

--- a/solution.py
+++ b/solution.py
@@ -8,9 +8,7 @@
 from jax.sharding import PartitionSpec as P
 
 MESH = pl.DeviceIdType.MESH
-BACKY_FIRST = True
 DY_AT = 1
-Y_EARLY = True
 GROUPS = 4
 EXPERTS = 32
 CAP = 10
@@ -207,20 +205,16 @@
 
     lax.fori_loop(0, CHUNKS, send_x, 0)
 
-    def send_dy(k, carry):
+    def send_dy(k):
         weight = jnp.sum(og[k], axis=1, keepdims=True)
         to_slabs(sy, k, dot(oh[k], tc[...].reshape(GROUPS * TOK, width)) * weight)
         send_slabs(sy, ry, sy_s, sy_r, k, 1)
-        return carry
 
     def await_cot():
         for p in range(1, GROUPS):
             dense(cotangent, tc, tc_s, tc_r, p).wait()
         own_tc.wait()
 
-    if DY_AT < 0:
-        await_cot()
-        lax.fori_loop(0, CHUNKS, send_dy, 0)
     for w in weights:
         w.wait()
 
@@ -278,19 +272,6 @@
     def partial_sums(k, q, value):
         part[k, :, q] = value.astype(jnp.bfloat16).reshape(GROUPS, OWN, value.shape[1])
 
-    def in_turn(step, later):
-        def body(k, carry):
-            step(k)
-
-            @pl.when(k > 0)
-            def _():
-                later(k - 1)
-
-            return carry
-
-        lax.fori_loop(0, CHUNKS, body, 0)
-        later(CHUNKS - 1)
-
     def first(k):
         await_slabs(sx, rx, sx_s, sx_r, k, 1)
         for h in range(2):
@@ -299,54 +280,26 @@
         rs_start(k, 0)
         partial_sums(k, 1, dot(xs[k], wu[...]))
         rs_start(k, 1)
-        if DY_AT >= 0:
-            @pl.when(k == DY_AT)
-            def _():
-                await_cot()
-
-            @pl.when(k >= DY_AT)
-            def _():
-                send_dy(k - DY_AT, 0)
-
-    def first_later(k):
+
+    def first_add(k):
         rs_add(k, 0)
         rs_add(k, 1)
 
-    in_turn(first, first_later)
-    if DY_AT > 0:
-        lax.fori_loop(CHUNKS - DY_AT, CHUNKS, send_dy, 0)
-
-    def send_y(k):
-        y = dot(ag_whole(k, 0), wd[...])
-        await_sent(sx, rx, sx_s, sx_r, k, 1)
-        to_slabs(sx, k, y)
-        send_slabs(sx, by, bks_y, bkr_y, k, -1)
-
-    def second(k):
+    def first_total(k):
         gate_h, up_h = rs_total(k, 0), rs_total(k, 1)
         gu[k, 0] = gate_h
         gu[k, 1] = up_h
         act[0, k, d] = (gate_h * jax.nn.sigmoid(gate_h) * up_h).astype(jnp.bfloat16)
         ag_start(k, 0)
+
+    def second(k):
         await_slabs(sy, ry, sy_s, sy_r, k, 1)
         for h in range(2):
             ys[k, :, h * half : (h + 1) * half] = from_slabs(ry, k, h)
         partial_sums(k, 2, lax.dot_general(ys[k], wd[...], NT, preferred_element_type=jnp.float32))
         rs_start(k, 2)
 
-    def second_later(k):
-        ag_forward(k, 0)
-        rs_add(k, 2)
-        if Y_EARLY:
-            @pl.when(k > 0)
-            def _():
-                send_y(k - 1)
-
-    in_turn(second, second_later)
-    if Y_EARLY:
-        send_y(CHUNKS - 1)
-
-    def third(k):
+    def second_total(k):
         d_h = rs_total(k, 2)
         gate_h, up_h = gu[k, 0], gu[k, 1]
         sigma = jax.nn.sigmoid(gate_h)
@@ -354,54 +307,76 @@
         ag_start(k, 1)
         act[2, k, d] = (d_h * (gate_h * sigma)).astype(jnp.bfloat16)
         ag_start(k, 2)
-        if not Y_EARLY:
-            send_y(k)
-
-    def third_later(k):
+
+    def second_forward(k):
         ag_forward(k, 1)
         ag_forward(k, 2)
 
-    in_turn(third, third_later)
-
-    def fourth(k, carry):
+    def send_y(k):
+        y = dot(ag_whole(k, 0), wd[...])
+        await_sent(sx, rx, sx_s, sx_r, k, 1)
+        to_slabs(sx, k, y)
+        send_slabs(sx, by, bks_y, bkr_y, k, -1)
+
+    def send_dx(k):
         dx = lax.dot_general(ag_whole(k, 1), wg[...], NT, preferred_element_type=jnp.float32)
         dx += lax.dot_general(ag_whole(k, 2), wu[...], NT, preferred_element_type=jnp.float32)
         await_sent(sy, ry, sy_s, sy_r, k, 1)
         to_slabs(sy, k, dx)
         send_slabs(sy, bx, bks_x, bkr_x, k, -1)
-        return carry
-
-    lax.fori_loop(0, CHUNKS, fourth, 0)
-
-    def final(src, dst, s, r, p):
-        q = lax.rem(d + p, GROUPS)
-        own = dst.at[:, pl.ds(pl.multiple_of(d * width, width), width)]
-        return remote(src.at[q], own, s.at[p - 1], r.at[p - 1], ring(p))
-
-    def combine(buf, matrix, stage):
+
+    def final(src, dst, s, r, p, h):
+        cols = pl.ds(pl.multiple_of(d * width + h * half, half), half)
+        out = src.at[lax.rem(d + p, GROUPS), :, pl.ds(h * half, half)]
+        return remote(out, dst.at[:, cols], s.at[p - 1, h], r.at[p - 1, h], ring(p))
+
+    def combine(buf, arrived, matrix, stage, dst, s, r):
         for h in range(2):
             total = jnp.zeros((GROUPS * TOK, half), jnp.float32)
             for k in range(CHUNKS):
+                if h == 0:
+                    await_bytes(buf, arrived, jnp.int32(k))
                 total += lax.dot_general(matrix(k), from_slabs(buf, k, h), TN, preferred_element_type=jnp.float32)
             stage[:, :, h * half : (h + 1) * half] = total.astype(jnp.bfloat16).reshape(GROUPS, TOK, half)
+            for p in (2, 1, 3):
+                final(stage, dst, s, r, p, h).start()
 
     def own_out(src, dst, sem):
         return pltpu.make_async_copy(src.at[d], dst.at[:, columns(0)], sem)
 
     def finish_y():
-        def back_y(k, carry):
-            await_slabs(sx, by, bks_y, bkr_y, k, -1)
-            await_sent(sx, by, bks_y, bkr_y, k, -1)
-            return carry
-
-        lax.fori_loop(0, CHUNKS, back_y, 0)
-        combine(by, lambda k: og[k].astype(jnp.bfloat16), tx)
-        for p in range(1, GROUPS):
-            final(tx, mixed, fm_s, fm_r, p).start()
+        combine(by, bkr_y, lambda k: og[k].astype(jnp.bfloat16), tx, mixed, fm_s, fm_r)
         own_out(tx, mixed, loc.at[0]).start()
 
-    if BACKY_FIRST:
-        finish_y()
+    stages = (
+        (0, first),
+        (DY_AT, send_dy),
+        (1, first_add),
+        (2, first_total),
+        (3, lambda k: ag_forward(k, 0)),
+        (4, send_y),
+        (5, lambda k: rs_add(k, 2)),
+        (6, second_total),
+        (7, second_forward),
+        (8, send_dx),
+        (4, second),
+    )
+    last = CHUNKS - 1 + max(lag for lag, _ in stages)
+
+    def step(now, carry):
+        @pl.when(now == DY_AT)
+        def _():
+            await_cot()
+
+        @pl.when(now == last)
+        def _():
+            finish_y()
+
+        for lag, stage in stages:
+            pl.when((now >= lag) & (now < lag + CHUNKS))(functools.partial(stage, now - lag))
+        return carry
+
+    lax.fori_loop(0, last + 1, step, 0)
 
     block = 256
 
@@ -433,26 +408,23 @@
     lax.fori_loop(0, width // block, down_grads, 0)
     outs[2].start()
 
-    if not BACKY_FIRST:
-        finish_y()
-
-    def back_x(k, carry):
-        await_slabs(sy, bx, bks_x, bkr_x, k, -1)
-        await_sent(sy, bx, bks_x, bkr_x, k, -1)
-        return carry
-
-    lax.fori_loop(0, CHUNKS, back_x, 0)
-    combine(bx, lambda k: oh[k], tc)
-    for p in range(1, GROUPS):
-        final(tc, d_tokens, fd_s, fd_r, p).start()
+    combine(bx, bkr_x, lambda k: oh[k], tc, d_tokens, fd_s, fd_r)
     own_out(tc, d_tokens, loc.at[1]).start()
     for p in range(1, GROUPS):
-        final(tx, mixed, fm_s, fm_r, p).wait()
-        final(tc, d_tokens, fd_s, fd_r, p).wait()
+        for h in range(2):
+            final(tx, mixed, fm_s, fm_r, p, h).wait()
+            final(tc, d_tokens, fd_s, fd_r, p, h).wait()
     own_out(tx, mixed, loc.at[0]).wait()
     own_out(tc, d_tokens, loc.at[1]).wait()
     for o in outs:
         o.wait()
+
+    def back_sent(k, carry):
+        await_bytes(sx, bks_y, k)
+        await_bytes(sy, bks_x, k)
+        return carry
+
+    lax.fori_loop(0, CHUNKS, back_sent, 0)
     sums, gathers = part.at[pl.ds(0, 3)], act.at[:, pl.ds(0, 3)]
     pltpu.make_async_copy(sums, sums, rs_s.at[0]).wait()
     pltpu.make_async_copy(gathers, gathers, ag_s.at[0]).wait()
@@ -506,23 +478,23 @@
         ]
         + [sem((CHUNKS,))] * 8
         + [sem((1,)), sem((CHUNKS, 3, 2)), sem((1,)), sem((CHUNKS, 3, 2))]
-        + [sem((3,))] * 4,
+        + [sem((3, 2))] * 4,
         compiler_params=pltpu.CompilerParams(
             collective_id=0, has_side_effects=True, vmem_limit_bytes=62 * 2**20
         ),
         cost_estimate=pl.CostEstimate(flops=24 * 10**9, bytes_accessed=14 * 10**6, transcendentals=500000),
     )(tab, tokens, cotangent, w_gate, w_up, w_down)
     specs = [
-        pl.BlockSpec((16, 4096), lambda i: (i, 0)),
-        pl.BlockSpec((16, 4096), lambda i: (i, 0)),
-        pl.BlockSpec((1, 128, 768), lambda i: (0, i, 0)),
-        pl.BlockSpec((1, 128, 768), lambda i: (0, i, 0)),
-        pl.BlockSpec((1, 96, 1024), lambda i: (0, i, 0)),
+        pl.BlockSpec((32, 4096), lambda i: (i, 0)),
+        pl.BlockSpec((32, 4096), lambda i: (i, 0)),
+        pl.BlockSpec((1, 256, 768), lambda i: (0, i, 0)),
+        pl.BlockSpec((1, 256, 768), lambda i: (0, i, 0)),
+        pl.BlockSpec((1, 192, 1024), lambda i: (0, i, 0)),
     ]
     return pl.pallas_call(
         publish,
         out_shape=[jax.ShapeDtypeStruct(r.shape, r.dtype) for r in results],
-        grid=(8,),
+        grid=(4,),
         in_specs=specs,
         out_specs=specs,
     )(*results)

time: 198 us -> 179 us (0.904); the launches traced: 197 us -> 176 us
  Pallas kernels: 195 us -> 174 us
    pallas_call x1, Pallas kernels: 187 us -> 168 us  [shards(): pl.pallas_call(kernel, out_shape=(jax.ShapeDtypeStruct(tokens.shape, bf16...]
where the time goes in v3:
time: 179 us; the launch traced here: 176 us
  Pallas kernels  174 us (97%)
  other arithmetic  1.94 us (1%)
    pallas_call x1, Pallas kernels, shards(): pl.pallas_call(kernel, out_shape=(jax.ShapeDtypeStruct(tokens.shape, bf16...  168 us
    pallas_call x1, Pallas kernels, shards(): pl.pallas_call(publish, out_shape=[jax.ShapeDtypeStruct(r.shape, r.dtype)...  6.1 us

profile of v3, /device:TPU:1, one launch (start us, length us, event | category | flops | bytes accessed | tf_op | source)
XLA Modules:
  0.0 176.5 jit_solution(7054797827114810806)
XLA Ops:
  0.6 0.7 convert_element_type.3
  1.3 1.3 maximum_bitcast_fusion.tab_ref
  2.6 167.8 %shard_map.110 = (bf16[128,4096]{1,0:T(8,128)(2,1)}, bf16[128,4096]{1,0:T(8,128)(2,1)}, bf16[1,1024,768]{2,1,0:T(8,128)(2,1)}, bf16[1,1024,768]{2,1,0:T(8,128)(2,1)}, bf16[1,768,1024]{2,1,0:T(8,128)(2,1)}) custom-call(f32[4,128]{1,0:T(4,128)} %maximum_bitcast_fusion.tab_ref, bf16[128,4096]{1,0:T(8,128)(2,1)} %tokens.1, bf16[128,4096]{1,0:T(8,128)(2,1)} %cotangent.1, ...), custom_call_target="tpu_custom_call" | custom-call | flops 24000000000 | bytes 14000000 | tf_op jit(solution)/shard_map/pallas_call | solution.py:448
  170.4 6.1 %shard_map.111 = (bf16[128,4096]{1,0:T(8,128)(2,1)}, bf16[128,4096]{1,0:T(8,128)(2,1)}, bf16[1,1024,768]{2,1,0:T(8,128)(2,1)}, bf16[1,1024,768]{2,1,0:T(8,128)(2,1)}, bf16[1,768,1024]{2,1,0:T(8,128)(2,1)}) custom-call(bf16[128,4096]{1,0:T(8,128)(2,1)} %get-tuple-element.10.refs_0_, bf16[128,4096]{1,0:T(8,128)(2,1)} %get-tuple-element.11.refs_1_, ...), custom_call_target="tpu_custom_call" | custom-call | tf_op jit(solution)/shard_map/pallas_call | solution.py:494

commit v4 on v3

--- a/solution.py
+++ b/solution.py
@@ -354,12 +354,12 @@
         (1, first_add),
         (2, first_total),
         (3, lambda k: ag_forward(k, 0)),
+        (4, second),
         (4, send_y),
         (5, lambda k: rs_add(k, 2)),
         (6, second_total),
         (7, second_forward),
         (8, send_dx),
-        (4, second),
     )
     last = CHUNKS - 1 + max(lag for lag, _ in stages)
 
@@ -431,8 +431,16 @@
 
 
 def publish(*refs):
-    for i in range(5):
-        refs[5 + i][...] = refs[i][...]
+    sources, targets, held, (come, go) = refs[:5], refs[5:10], refs[10:15], refs[15:]
+    reads = [pltpu.make_async_copy(sources[i], held[i], come.at[i]) for i in range(5)]
+    writes = [pltpu.make_async_copy(held[i], targets[i], go.at[i]) for i in range(5)]
+    for read in reads:
+        read.start()
+    for read, write in zip(reads, writes):
+        read.wait()
+        write.start()
+    for write in writes:
+        write.wait()
 
 
 def shards(tokens, routes, gates, cotangent, w_gate, w_up, w_down):
@@ -484,19 +492,13 @@
         ),
         cost_estimate=pl.CostEstimate(flops=24 * 10**9, bytes_accessed=14 * 10**6, transcendentals=500000),
     )(tab, tokens, cotangent, w_gate, w_up, w_down)
-    specs = [
-        pl.BlockSpec((32, 4096), lambda i: (i, 0)),
-        pl.BlockSpec((32, 4096), lambda i: (i, 0)),
-        pl.BlockSpec((1, 256, 768), lambda i: (0, i, 0)),
-        pl.BlockSpec((1, 256, 768), lambda i: (0, i, 0)),
-        pl.BlockSpec((1, 192, 1024), lambda i: (0, i, 0)),
-    ]
     return pl.pallas_call(
         publish,
         out_shape=[jax.ShapeDtypeStruct(r.shape, r.dtype) for r in results],
-        grid=(4,),
-        in_specs=specs,
-        out_specs=specs,
+        in_specs=[hbm] * 5,
+        out_specs=[hbm] * 5,
+        scratch_shapes=[pltpu.VMEM(r.shape, r.dtype) for r in results] + [sem((5,)), sem((5,))],
+        compiler_params=pltpu.CompilerParams(vmem_limit_bytes=62 * 2**20),
     )(*results)
 
 

time: 179 us -> 177 us (0.989)
  no operation moved by 1% of the time
where the time goes in v4:
time: 177 us; the launch traced here: 176 us
  Pallas kernels  173 us (98%)
  other arithmetic  1.94 us (1%)
    pallas_call x1, Pallas kernels, shards(): pl.pallas_call(kernel, out_shape=(jax.ShapeDtypeStruct(tokens.shape, bf16...  168 us
    pallas_call x1, Pallas kernels, shards(): pl.pallas_call(publish, out_shape=[jax.ShapeDtypeStruct(r.shape, r.dtype)...  5.55 us

profile of v4, /device:TPU:1, one launch (start us, length us, event | category | flops | bytes accessed | tf_op | source)
XLA Modules:
  0.0 175.8 jit_solution(739027470703402901)
XLA Ops:
  0.6 0.7 convert_element_type.3
  1.3 1.3 maximum_bitcast_fusion.tab_ref
  2.6 167.7 %shard_map.110 = (bf16[128,4096]{1,0:T(8,128)(2,1)}, bf16[128,4096]{1,0:T(8,128)(2,1)}, bf16[1,1024,768]{2,1,0:T(8,128)(2,1)}, bf16[1,1024,768]{2,1,0:T(8,128)(2,1)}, bf16[1,768,1024]{2,1,0:T(8,128)(2,1)}) custom-call(f32[4,128]{1,0:T(4,128)} %maximum_bitcast_fusion.tab_ref, bf16[128,4096]{1,0:T(8,128)(2,1)} %tokens.1, bf16[128,4096]{1,0:T(8,128)(2,1)} %cotangent.1, ...), custom_call_target="tpu_custom_call" | custom-call | flops 24000000000 | bytes 14000000 | tf_op jit(solution)/shard_map/pallas_call | solution.py:456
  170.3 5.5 %shard_map.111 = (bf16[128,4096]{1,0:T(8,128)(2,1)}, bf16[128,4096]{1,0:T(8,128)(2,1)}, bf16[1,1024,768]{2,1,0:T(8,128)(2,1)}, bf16[1,1024,768]{2,1,0:T(8,128)(2,1)}, bf16[1,768,1024]{2,1,0:T(8,128)(2,1)}) custom-call(bf16[128,4096]{1,0:T(8,128)(2,1)} %get-tuple-element.10.refs_0_, bf16[128,4096]{1,0:T(8,128)(2,1)} %get-tuple-element.11.refs_1_, ...), custom_call_target="tpu_custom_call" | custom-call | tf_op jit(solution)/shard_map/pallas_call | solution.py:495

commit v5 on v4

--- a/solution.py
+++ b/solution.py
@@ -120,9 +120,9 @@
 
     own_tx = pltpu.make_async_copy(tokens.at[:, columns(0)], tx.at[d], loc.at[0])
     own_tc = pltpu.make_async_copy(cotangent.at[:, columns(0)], tc.at[d], loc.at[1])
-    for p in range(1, GROUPS):
+    own_tx.start()
+    for p in (2, 1, 3):
         dense(tokens, tx, tx_s, tx_r, p).start()
-    own_tx.start()
     for p in range(1, GROUPS):
         dense(cotangent, tc, tc_s, tc_r, p).start()
     own_tc.start()
@@ -383,6 +383,22 @@
     def all_rows(q):
         return act[q].reshape(CHUNKS * ROWS, act.shape[4])
 
+    outs = [
+        pltpu.make_async_copy(gg.at[0], g_gate.at[0], loc.at[2]),
+        pltpu.make_async_copy(gg.at[1], g_up.at[0], loc.at[3]),
+        pltpu.make_async_copy(wd, g_down.at[0], loc.at[4]),
+    ]
+    def down_grads(b, carry):
+        cols = pl.ds(pl.multiple_of(b * block, block), block)
+        dy = ys[:, :, cols].reshape(CHUNKS * ROWS, block)
+        wd[:, cols] = lax.dot_general(all_rows(0), dy, TN, preferred_element_type=jnp.float32).astype(jnp.bfloat16)
+        return carry
+
+    lax.fori_loop(0, width // block, down_grads, 0)
+    outs[2].start()
+
+    combine(bx, bkr_x, lambda k: oh[k], tc, d_tokens, fd_s, fd_r)
+    own_out(tc, d_tokens, loc.at[1]).start()
     def weight_grads(b, carry):
         cols = pl.ds(pl.multiple_of(b * block, block), block)
         x = xs[:, :, cols].reshape(CHUNKS * ROWS, block)
@@ -391,25 +407,8 @@
         return carry
 
     lax.fori_loop(0, width // block, weight_grads, 0)
-    outs = [
-        pltpu.make_async_copy(gg.at[0], g_gate.at[0], loc.at[2]),
-        pltpu.make_async_copy(gg.at[1], g_up.at[0], loc.at[3]),
-        pltpu.make_async_copy(wd, g_down.at[0], loc.at[4]),
-    ]
     outs[0].start()
     outs[1].start()
-
-    def down_grads(b, carry):
-        cols = pl.ds(pl.multiple_of(b * block, block), block)
-        dy = ys[:, :, cols].reshape(CHUNKS * ROWS, block)
-        wd[:, cols] = lax.dot_general(all_rows(0), dy, TN, preferred_element_type=jnp.float32).astype(jnp.bfloat16)
-        return carry
-
-    lax.fori_loop(0, width // block, down_grads, 0)
-    outs[2].start()
-
-    combine(bx, bkr_x, lambda k: oh[k], tc, d_tokens, fd_s, fd_r)
-    own_out(tc, d_tokens, loc.at[1]).start()
     for p in range(1, GROUPS):
         for h in range(2):
             final(tx, mixed, fm_s, fm_r, p, h).wait()

time: 177 us -> 177 us (level)
  no operation moved by 1% of the time
where the time goes in v5:
time: 177 us; the launch traced here: 176 us
  Pallas kernels  173 us (98%)
  other arithmetic  1.94 us (1%)
    pallas_call x1, Pallas kernels, shards(): pl.pallas_call(kernel, out_shape=(jax.ShapeDtypeStruct(tokens.shape, bf16...  168 us
    pallas_call x1, Pallas kernels, shards(): pl.pallas_call(publish, out_shape=[jax.ShapeDtypeStruct(r.shape, r.dtype)...  5.55 us

profile of v5, /device:TPU:1, one launch (start us, length us, event | category | flops | bytes accessed | tf_op | source)
XLA Modules:
  0.0 175.6 jit_solution(12808393324390553249)
XLA Ops:
  0.6 0.7 convert_element_type.3
  1.3 1.3 maximum_bitcast_fusion.tab_ref
  2.6 167.5 %shard_map.110 = (bf16[128,4096]{1,0:T(8,128)(2,1)}, bf16[128,4096]{1,0:T(8,128)(2,1)}, bf16[1,1024,768]{2,1,0:T(8,128)(2,1)}, bf16[1,1024,768]{2,1,0:T(8,128)(2,1)}, bf16[1,768,1024]{2,1,0:T(8,128)(2,1)}) custom-call(f32[4,128]{1,0:T(4,128)} %maximum_bitcast_fusion.tab_ref, bf16[128,4096]{1,0:T(8,128)(2,1)} %tokens.1, bf16[128,4096]{1,0:T(8,128)(2,1)} %cotangent.1, ...), custom_call_target="tpu_custom_call" | custom-call | flops 24000000000 | bytes 14000000 | tf_op jit(solution)/shard_map/pallas_call | solution.py:455
  170.1 5.5 %shard_map.111 = (bf16[128,4096]{1,0:T(8,128)(2,1)}, bf16[128,4096]{1,0:T(8,128)(2,1)}, bf16[1,1024,768]{2,1,0:T(8,128)(2,1)}, bf16[1,1024,768]{2,1,0:T(8,128)(2,1)}, bf16[1,768,1024]{2,1,0:T(8,128)(2,1)}) custom-call(bf16[128,4096]{1,0:T(8,128)(2,1)} %get-tuple-element.10.refs_0_, bf16[128,4096]{1,0:T(8,128)(2,1)} %get-tuple-element.11.refs_1_, ...), custom_call_target="tpu_custom_call" | custom-call | tf_op jit(solution)/shard_map/pallas_call | solution.py:494
